TPU v7x, 32 devices: a whole 2x2x4 slice. The times are simulated.
32 devices in a mesh: dp: 8 (over z, x), group: 4 (over y, core).
Axes of the slice: x: 2, y: 2, z: 4, core: 2. Of those that a mesh axis runs over, the one named last changes fastest.
Arguments:
- enc: bfloat16 [36864, 512], P(('dp', 'group')), may hold values from -6 to 6
- visible: int32 [36864], P(('dp', 'group')), may hold values 0 or 1
- band_group: int32 [36864], P(('dp', 'group')), may hold values from 0 to 3, as said below
- cotangent: bfloat16 [36864, 512], P(('dp', 'group')), may hold values from -6 to 6
- ln1_gain: float32 [512], replicated, may hold values from 0.5 to 1.5
- ln1_bias: float32 [512], replicated, may hold values from -3 to 3
- w_qkv: bfloat16 [512, 1536], replicated, may hold values from -0.25 to 0.25
- w_out: bfloat16 [512, 512], replicated, may hold values from -1.5 to 1.5
- ln2_gain: float32 [512], replicated, may hold values from 0.5 to 1.5
- ln2_bias: float32 [512], replicated, may hold values from -3 to 3
- w_up: bfloat16 [512, 2048], replicated, may hold values from -0.25 to 0.25
- w_down: bfloat16 [2048, 512], replicated, may hold values from -0.125 to 0.125
- mask_token: float32 [512], replicated, may hold values from -5 to 5
Outputs:
- out: bfloat16 [36864, 512], P(('dp', 'group'))
- grad_enc: bfloat16 [36864, 512], P(('dp', 'group'))
- grad_ln1_gain: float32 [512], replicated
- grad_ln1_bias: float32 [512], replicated
- grad_w_qkv: float32 [512, 1536], replicated
- grad_w_out: float32 [512, 512], replicated
- grad_ln2_gain: float32 [512], replicated
- grad_ln2_bias: float32 [512], replicated
- grad_w_up: float32 [512, 2048], replicated
- grad_w_down: float32 [2048, 512], replicated
- grad_mask_token: float32 [512], replicated
Inputs may be any that keep to these rules, and one draw needn't show every extreme that they name: `band_group`: in every cube, each device's 384 tokens of it hold at most 128 tokens of any one band group, and one band group of the cube has exactly 128 on every device.
All inputs are finite; a program needn't handle non-finite values. No bound on the sum of `visible` on one device may be relied on, other than what follows from the above.
Results may differ from a plain program's by a relative error of at most 0.013.
Values may be sent and summed in bfloat16 or wider, within the bound.
A program may use at most 192 MiB of HBM per device.

v0:
```python
import jax
import jax.numpy as jnp
from jax import lax
from jax.sharding import PartitionSpec as P

HEADS = 16
CUBE_TOK = 1536


EPS = 1e-05
NEG = -1e30


def norm_stats(values):
    centre = values - jnp.mean(values, axis=-1, keepdims=True)
    spread = jnp.mean(centre * centre, axis=-1, keepdims=True)
    recip = lax.rsqrt(spread + EPS)
    return (centre * recip, recip)


def norm_back(grad_rows, normal, recip, gain):
    scaled = grad_rows * gain
    return recip * (
        scaled
        - jnp.mean(scaled, axis=-1, keepdims=True)
        - normal * jnp.mean(scaled * normal, axis=-1, keepdims=True)
    )


def inner_rows(left, right):
    return lax.dot_general(
        left, right, (((0,), (0,)), ((), ())), preferred_element_type=jnp.float32
    )


def outer_cols(left, right):
    return lax.dot_general(
        left, right, (((1,), (1,)), ((), ())), preferred_element_type=jnp.float32
    )


def gelu_fn(values):
    return jax.nn.gelu(values, approximate=True)


def split_heads(packed):
    width = packed.shape[1] // 3
    head_dim = width // HEADS
    queries = packed[:, :width].reshape(-1, HEADS, head_dim)
    key_rows = packed[:, width : 2 * width].reshape(-1, HEADS, head_dim)
    value_rows = packed[:, 2 * width :].reshape(-1, HEADS, head_dim)
    return (queries, key_rows, value_rows, head_dim ** (-0.5))


def score_block(queries, key_rows, live, factor):
    scores = (
        jnp.einsum("qhd,khd->hqk", queries, key_rows, preferred_element_type=jnp.float32) * factor
    )
    return jnp.where(live[None, None, :], scores, NEG)


def attend(packed, live):
    queries, key_rows, value_rows, factor = split_heads(packed)
    scores = score_block(queries, key_rows, live, factor)
    top = jnp.max(scores, axis=-1, keepdims=True)
    expo = jnp.exp(scores - top)
    total = jnp.sum(expo, axis=-1, keepdims=True)
    probs = expo / total
    log_total = top[:, :, 0] + jnp.log(total[:, :, 0])
    attended = jnp.einsum(
        "hqk,khd->qhd", probs.astype(jnp.bfloat16), value_rows, preferred_element_type=jnp.float32
    )
    return (attended.reshape(packed.shape[0], -1).astype(jnp.bfloat16), log_total)


def attend_back(packed, live, log_total, grad_rows):
    queries, key_rows, value_rows, factor = split_heads(packed)
    scores = score_block(queries, key_rows, live, factor)
    probs = jnp.exp(scores - log_total[:, :, None])
    grad_heads = grad_rows.reshape(queries.shape)
    grad_values = jnp.einsum(
        "hqk,qhd->khd", probs.astype(jnp.bfloat16), grad_heads, preferred_element_type=jnp.float32
    ).astype(jnp.bfloat16)
    grad_probs = jnp.einsum(
        "qhd,khd->hqk", grad_heads, value_rows, preferred_element_type=jnp.float32
    )
    centred = jnp.sum(probs * grad_probs, axis=-1, keepdims=True)
    grad_scores = (probs * (grad_probs - centred)).astype(jnp.bfloat16)
    grad_queries = (
        jnp.einsum("hqk,khd->qhd", grad_scores, key_rows, preferred_element_type=jnp.float32)
        * factor
    ).astype(jnp.bfloat16)
    grad_keys = (
        jnp.einsum("hqk,qhd->khd", grad_scores, queries, preferred_element_type=jnp.float32)
        * factor
    ).astype(jnp.bfloat16)
    rows = packed.shape[0]
    return jnp.concatenate(
        [
            grad_queries.reshape(rows, -1),
            grad_keys.reshape(rows, -1),
            grad_values.reshape(rows, -1),
        ],
        axis=1,
    )


def on_device(
    enc,
    visible,
    band_group,
    cotangent,
    ln1_gain,
    ln1_bias,
    w_qkv,
    w_out,
    ln2_gain,
    ln2_bias,
    w_up,
    w_down,
    mask_token,
):
    groups = lax.axis_size("group")
    owner_index = lax.axis_index("group")
    tok_dev, width = enc.shape
    quarter = CUBE_TOK // groups
    capacity = quarter // 3
    cubes = tok_dev // quarter
    set_rows = capacity * groups
    local_ids = band_group.reshape(cubes, quarter)
    onehot = (local_ids[:, :, None] == jnp.arange(groups, dtype=jnp.int32)[None, None, :]).astype(
        jnp.int32
    )
    ranks = jnp.sum((jnp.cumsum(onehot, axis=1) - onehot) * onehot, axis=-1)
    destination = (
        (jnp.arange(cubes, dtype=jnp.int32)[:, None] * groups + local_ids) * capacity + ranks
    ).reshape(tok_dev)

    def dispatch(rows):
        buffer = (
            jnp.zeros((cubes * groups * capacity, rows.shape[1]), rows.dtype)
            .at[destination]
            .set(rows)
        )
        return buffer.reshape(cubes, groups, capacity, rows.shape[1])

    def collect(buffer):
        return buffer.reshape(cubes * groups * capacity, -1)[destination]

    all_ids = lax.all_gather(band_group, "group", axis=0, tiled=True).reshape(
        groups, cubes, quarter
    )
    counts = jnp.sum((all_ids == owner_index).astype(jnp.int32), axis=-1).T
    live = (jnp.arange(capacity, dtype=jnp.int32)[None, None, :] < counts[:, :, None]).reshape(
        cubes, set_rows
    )
    shown = (visible == 1)[:, None]
    start_rows = jnp.where(shown, enc.astype(jnp.float32), mask_token[None, :])
    normal1, recip1 = norm_stats(start_rows)
    normed = (normal1 * ln1_gain + ln1_bias).astype(jnp.bfloat16)
    projected = jnp.dot(normed, w_qkv, preferred_element_type=jnp.float32).astype(jnp.bfloat16)
    owner_rows = lax.all_to_all(
        dispatch(projected), "group", split_axis=1, concat_axis=1, tiled=True
    ).reshape(cubes, set_rows, 3 * width)
    owner_attended, log_totals = lax.map(
        lambda items: attend(items[0], items[1]), (owner_rows, live)
    )
    returned = lax.all_to_all(
        owner_attended.reshape(cubes, groups, capacity, width),
        "group",
        split_axis=1,
        concat_axis=1,
        tiled=True,
    )
    attended = collect(returned)
    middle = start_rows + jnp.dot(attended, w_out, preferred_element_type=jnp.float32)
    normal2, recip2 = norm_stats(middle)
    second = (normal2 * ln2_gain + ln2_bias).astype(jnp.bfloat16)
    hidden = jnp.dot(second, w_up, preferred_element_type=jnp.float32)
    active_full, gelu_pull = jax.vjp(gelu_fn, hidden)
    active = active_full.astype(jnp.bfloat16)
    out = (middle + jnp.dot(active, w_down, preferred_element_type=jnp.float32)).astype(
        jnp.bfloat16
    )
    grad_w_down = inner_rows(active, cotangent)
    grad_active = outer_cols(cotangent, w_down)
    grad_hidden = gelu_pull(grad_active)[0].astype(jnp.bfloat16)
    grad_w_up = inner_rows(second, grad_hidden)
    grad_second = outer_cols(grad_hidden, w_up)
    grad_ln2_gain = jnp.sum(grad_second * normal2, axis=0)
    grad_ln2_bias = jnp.sum(grad_second, axis=0)
    grad_middle = cotangent.astype(jnp.float32) + norm_back(grad_second, normal2, recip2, ln2_gain)
    grad_branch = grad_middle.astype(jnp.bfloat16)
    grad_w_out = inner_rows(attended, grad_branch)
    grad_attended = outer_cols(grad_branch, w_out).astype(jnp.bfloat16)
    owner_grads = lax.all_to_all(
        dispatch(grad_attended), "group", split_axis=1, concat_axis=1, tiled=True
    ).reshape(cubes, set_rows, width)
    grad_sets = lax.map(
        lambda items: attend_back(items[0], items[1], items[2], items[3]),
        (owner_rows, live, log_totals, owner_grads),
    )
    grad_projected = collect(
        lax.all_to_all(
            grad_sets.reshape(cubes, groups, capacity, 3 * width),
            "group",
            split_axis=1,
            concat_axis=1,
            tiled=True,
        )
    )
    grad_w_qkv = inner_rows(normed, grad_projected)
    grad_normed = outer_cols(grad_projected, w_qkv).astype(jnp.bfloat16)
    grad_normed_full = grad_normed.astype(jnp.float32)
    grad_ln1_gain = jnp.sum(grad_normed_full * normal1, axis=0)
    grad_ln1_bias = jnp.sum(grad_normed_full, axis=0)
    grad_start = grad_middle + norm_back(grad_normed_full, normal1, recip1, ln1_gain)
    grad_enc = jnp.where(shown, grad_start, 0.0).astype(jnp.bfloat16)
    grad_mask_token = jnp.sum(jnp.where(shown, 0.0, grad_start), axis=0)
    summed = lax.psum(
        (
            grad_ln1_gain,
            grad_ln1_bias,
            grad_w_qkv,
            grad_w_out,
            grad_ln2_gain,
            grad_ln2_bias,
            grad_w_up,
            grad_w_down,
            grad_mask_token,
        ),
        ("dp", "group"),
    )
    return (
        out,
        grad_enc,
        summed[0],
        summed[1],
        summed[2],
        summed[3],
        summed[4],
        summed[5],
        summed[6],
        summed[7],
        summed[8],
    )


def solution(mesh):
    placed = (
        P(("dp", "group"), None),
        P(("dp", "group")),
        P(("dp", "group")),
        P(("dp", "group"), None),
        P(),
        P(),
        P(),
        P(),
        P(),
        P(),
        P(),
        P(),
        P(),
    )
    return jax.shard_map(
        on_device,
        mesh=mesh,
        in_specs=placed,
        out_specs=(
            P(("dp", "group"), None),
            P(("dp", "group"), None),
            P(),
            P(),
            P(),
            P(),
            P(),
            P(),
            P(),
            P(),
            P(),
        ),
        check_vma=False,
    )
```

profile of v0, /device:TPU:0, one launch (start us, length us, event | category | flops | bytes accessed | tf_op | source)
XLA Modules:
  0.0 739.4 jit_solution(16594753733006182318)
XLA Ops:
  9.6 3.6 reduce-window.6
  17.8 4.1 convolution_convert_fusion
  21.9 12.2 %scatter_custom_fusion = bf16[1536,1536]{1,0:T(8,128)(2,1)} fusion(s32[1152]{0:T(1024)S(1)} %compare_select_fusion, bf16[1152,1536]{1,0:T(8,128)(2,1)} %convolution_convert_fusion, bf16[]{:T(256)} %constant.48.clone.1), kind=kCustom, calls=%fused_computation.69 | custom fusion | bytes 4719104 | tf_op jit(solution)/shard_map/scatter | solution.py:143
  34.1 4.8 copy.103
  39.0 5.0 all-to-all-start
  44.0 55.4 %all-gather = s32[4,1,1152]{2,1,0:T(1,128)S(1)} all-gather(s32[1,1,1152]{2,1,0:T(1,128)S(1)} %reshape.236), channel_id=1, replica_groups=mesh['dp'=8,'group'=4] {'group'}, dimensions={0}, use_global_device_ids=true | all-gather | bytes 23040 | tf_op jit(solution)/shard_map/all_gather | solution.py:150
  99.6 4.8 copy.104
  104.4 6.6 copy.106
  111.0 44.9 %while.22 = (s32[]{:T(128)}, bf16[3,512,512]{2,1,0:T(8,128)(2,1)}, f32[3,16,512]{2,1,0:T(8,128)S(1)}, bf16[3,512,1536]{1,2,0:T(8,128)(2,1)}, pred[3,512]{1,0:T(4,128)(4,1)S(1)}, /*index=5*/s32[]{:T(128)}) while((s32[]{:T(128)}, bf16[3,512,512]{2,1,0:T(8,128)(2,1)}, f32[3,16,512]{2,1,0:T(8,128)S(1)}, bf16[3,512,1536]{1,2,0:T(8,128)(2,1)}, ...), condition=%wide.region_10.11_spmd, body=%wide.region_7.10_spmd.sunk | while | flops 587456512 | bytes 61082204 | solution.py:165
  112.7 4.3 fusion.107
  117.0 3.8 fusion.108
  120.8 4.1 fusion.109
  127.6 4.3 fusion.107
  131.9 3.8 fusion.108
  135.8 4.1 fusion.109
  142.6 4.3 fusion.107
  146.9 3.8 fusion.108
  150.7 4.1 fusion.109
  155.9 2.7 copy.108
  158.6 15.6 %all-to-all-start.1 = ((bf16[3,4,128,512]{3,2,0,1:T(8,128)(2,1)}), bf16[3,4,128,512]{3,2,0,1:T(8,128)(2,1)}, u32[]{:S(2)}, u32[]{:S(2)}) async-start(bf16[3,4,128,512]{3,2,0,1:T(8,128)(2,1)} %copy.108), calls=%async_computation.1 | async-start | bytes 3145728 | tf_op jit(solution)/shard_map/all_to_all | solution.py:168
  175.6 18.5 %all-to-all-done.1 = bf16[3,4,128,512]{3,2,0,1:T(8,128)(2,1)} async-done(((bf16[3,4,128,512]{3,2,0,1:T(8,128)(2,1)}), bf16[3,4,128,512]{3,2,0,1:T(8,128)(2,1)}, u32[]{:S(2)}, u32[]{:S(2)}) %all-to-all-start.1) | async-done | bytes 1572896 | tf_op jit(solution)/shard_map/all_to_all | solution.py:168
  194.0 2.7 copy.109
  196.7 6.4 gather_fusion
  206.9 2.9 fusion.44
  209.8 8.3 %fusion.19 = bf16[1152,2048]{1,0:T(8,128)(2,1)S(1)} fusion(f32[1152,2048]{1,0:T(8,128)S(1)} %fusion.44, bf16[1152,512]{1,0:T(8,128)(2,1)S(1)} %copy-done.22, bf16[2048,512]{1,0:T(8,128)(2,1)S(1)} %copy-done.53), kind=kOutput, calls=%fused_computation.41 | convolution fusion | flops 2463105024 | bytes 17432576 | tf_op jit(solution)/shard_map/dot_general | solution.py:37
  218.1 4.7 fusion.51
  222.8 3.1 copy.112
  225.9 3.8 multiply_reduce_fusion.1
  232.8 8.5 %scatter_custom_fusion.1 = bf16[1536,512]{1,0:T(8,128)(2,1)S(1)} fusion(s32[1152]{0:T(1024)S(1)} %copy-done.43, bf16[1152,512]{1,0:T(8,128)(2,1)S(1)} %convolution_convert_fusion.2, bf16[]{:T(256)} %constant.48.clone.1), kind=kCustom, calls=%fused_computation.77 | custom fusion | bytes 1572866 | tf_op jit(solution)/shard_map/scatter | solution.py:143
  242.5 4.8 all-to-all-start.2
  247.3 20.1 %all-to-all-done.2 = bf16[3,4,128,512]{3,2,0,1:T(8,128)(2,1)} async-done(((bf16[3,4,128,512]{3,2,0,1:T(8,128)(2,1)}), bf16[3,4,128,512]{3,2,0,1:T(8,128)(2,1)}, u32[]{:S(2)}, u32[]{:S(2)}) %all-to-all-start.2) | async-done | bytes 1572896 | tf_op jit(solution)/shard_map/all_to_all | solution.py:196
  268.9 132.3 %while.23 = (s32[]{:T(128)}, bf16[3,512,1536]{2,1,0:T(8,128)(2,1)}, bf16[3,512,1536]{1,2,0:T(8,128)(2,1)}, pred[3,512]{1,0:T(4,128)(4,1)S(1)}, f32[3,16,512]{2,1...) while((s32[]{:T(128)}, bf16[3,512,1536]{2,1,0:T(8,128)(2,1)}, ...), condition=%wide.region_18.19_spmd, body=%wide.region_16.18_spmd.sunk | while | flops 1385947136 | bytes 200312688 | solution.py:199
  273.3 2.4 fusion.121
  275.7 10.0 %multiply_reduce_fusion.7 = (f32[16,512]{1,0:T(8,128)S(1)}, f32[16,512,512]{1,2,0:T(8,128)}) fusion(f32[16,512,512]{1,2,0:T(8,128)S(1)} %fusion.121, f32[16,512]{1,0:T(8,128)S(1)} %copy-done.20, bf16[512,16,32]{0,2,1:T(8,128)(2,1)S(1)} %bitcast.141, bf16[512,16,32]{0,2,1:T(8,128)(2,1)S(1)} %bitcast.139, pred[512]{0:T(512)(128)(4,1)S(1)} %dynamic-slice_reduce_fusion.5), kind=kOutput, calls=%fused_computation.18.clone.1 | convolution fusion | flops 289398784 | bytes 34669056 | tf_op jit(solution)/shard_map/while/body/eval_jaxpr/qhd,khd->hqk/dot_general | solution.py:57
  285.6 10.6 %multiply_convert_fusion.5 = bf16[16,512,512]{1,2,0:T(8,128)(2,1)} fusion(f32[16,512,512]{1,2,0:T(8,128)} %get-tuple-element.307, f32[16,512,512]{1,2,0:T(8,128)S(1)} %fusion.121, f32[16,512]{1,0:T(8,128)S(1)} %get-tuple-element.308), kind=kLoop, calls=%fused_computation.17.clone.1 | loop fusion | flops 12582912 | bytes 41975808 | tf_op jit(solution)/shard_map/while/body/eval_jaxpr/convert_element_type | solution.py:88
  296.2 8.5 %fusion.122 = bf16[16,32,512]{2,1,0:T(8,128)(2,1)S(1)} fusion(bf16[512,16,32]{0,2,1:T(8,128)(2,1)S(1)} %bitcast.144, f32[16,512,512]{1,2,0:T(8,128)} %get-tuple-element.307), kind=kOutput, calls=%fused_computation.26.clone.1 | convolution fusion | flops 272891904 | bytes 17825792 | tf_op jit(solution)/shard_map/while/body/eval_jaxpr/hqk,qhd->khd/dot_general | solution.py:81
  306.0 2.5 fusion.123
  310.2 2.8 constant_dynamic-update-slice_fusion.5
  317.3 2.4 fusion.121
  319.7 10.0 %multiply_reduce_fusion.7 = (f32[16,512]{1,0:T(8,128)S(1)}, f32[16,512,512]{1,2,0:T(8,128)}) fusion(f32[16,512,512]{1,2,0:T(8,128)S(1)} %fusion.121, f32[16,512]{1,0:T(8,128)S(1)} %copy-done.20, bf16[512,16,32]{0,2,1:T(8,128)(2,1)S(1)} %bitcast.141, bf16[512,16,32]{0,2,1:T(8,128)(2,1)S(1)} %bitcast.139, pred[512]{0:T(512)(128)(4,1)S(1)} %dynamic-slice_reduce_fusion.5), kind=kOutput, calls=%fused_computation.18.clone.1 | convolution fusion | flops 289398784 | bytes 34669056 | tf_op jit(solution)/shard_map/while/body/eval_jaxpr/qhd,khd->hqk/dot_general | solution.py:57
  329.7 10.6 %multiply_convert_fusion.5 = bf16[16,512,512]{1,2,0:T(8,128)(2,1)} fusion(f32[16,512,512]{1,2,0:T(8,128)} %get-tuple-element.307, f32[16,512,512]{1,2,0:T(8,128)S(1)} %fusion.121, f32[16,512]{1,0:T(8,128)S(1)} %get-tuple-element.308), kind=kLoop, calls=%fused_computation.17.clone.1 | loop fusion | flops 12582912 | bytes 41975808 | tf_op jit(solution)/shard_map/while/body/eval_jaxpr/convert_element_type | solution.py:88
  340.3 8.5 %fusion.122 = bf16[16,32,512]{2,1,0:T(8,128)(2,1)S(1)} fusion(bf16[512,16,32]{0,2,1:T(8,128)(2,1)S(1)} %bitcast.144, f32[16,512,512]{1,2,0:T(8,128)} %get-tuple-element.307), kind=kOutput, calls=%fused_computation.26.clone.1 | convolution fusion | flops 272891904 | bytes 17825792 | tf_op jit(solution)/shard_map/while/body/eval_jaxpr/hqk,qhd->khd/dot_general | solution.py:81
  350.0 2.5 fusion.123
  354.3 2.8 constant_dynamic-update-slice_fusion.5
  361.4 2.4 fusion.121
  363.8 10.0 %multiply_reduce_fusion.7 = (f32[16,512]{1,0:T(8,128)S(1)}, f32[16,512,512]{1,2,0:T(8,128)}) fusion(f32[16,512,512]{1,2,0:T(8,128)S(1)} %fusion.121, f32[16,512]{1,0:T(8,128)S(1)} %copy-done.20, bf16[512,16,32]{0,2,1:T(8,128)(2,1)S(1)} %bitcast.141, bf16[512,16,32]{0,2,1:T(8,128)(2,1)S(1)} %bitcast.139, pred[512]{0:T(512)(128)(4,1)S(1)} %dynamic-slice_reduce_fusion.5), kind=kOutput, calls=%fused_computation.18.clone.1 | convolution fusion | flops 289398784 | bytes 34669056 | tf_op jit(solution)/shard_map/while/body/eval_jaxpr/qhd,khd->hqk/dot_general | solution.py:57
  373.8 10.6 %multiply_convert_fusion.5 = bf16[16,512,512]{1,2,0:T(8,128)(2,1)} fusion(f32[16,512,512]{1,2,0:T(8,128)} %get-tuple-element.307, f32[16,512,512]{1,2,0:T(8,128)S(1)} %fusion.121, f32[16,512]{1,0:T(8,128)S(1)} %get-tuple-element.308), kind=kLoop, calls=%fused_computation.17.clone.1 | loop fusion | flops 12582912 | bytes 41975808 | tf_op jit(solution)/shard_map/while/body/eval_jaxpr/convert_element_type | solution.py:88
  384.4 8.5 %fusion.122 = bf16[16,32,512]{2,1,0:T(8,128)(2,1)S(1)} fusion(bf16[512,16,32]{0,2,1:T(8,128)(2,1)S(1)} %bitcast.144, f32[16,512,512]{1,2,0:T(8,128)} %get-tuple-element.307), kind=kOutput, calls=%fused_computation.26.clone.1 | convolution fusion | flops 272891904 | bytes 17825792 | tf_op jit(solution)/shard_map/while/body/eval_jaxpr/hqk,qhd->khd/dot_general | solution.py:81
  394.1 2.5 fusion.123
  398.4 2.8 constant_dynamic-update-slice_fusion.5
  401.2 4.7 copy.118
  405.9 5.1 all-to-all-start.3
  411.3 3.7 fusion.36
  415.1 7.2 fusion.43
  422.3 5.3 fusion.46
  427.5 37.3 %all-to-all-done.3 = bf16[3,4,128,1536]{3,2,0,1:T(8,128)(2,1)} async-done(((bf16[3,4,128,1536]{3,2,0,1:T(8,128)(2,1)}), bf16[3,4,128,1536]{3,2,0,1:T(8,128)(2,1)}, u32[]{:S(2)}, u32[]{:S(2)}) %all-to-all-start.3) | async-done | bytes 4718624 | tf_op jit(solution)/shard_map/all_to_all | solution.py:204
  464.9 4.8 copy.119
  469.7 11.8 %gather_fusion.1 = bf16[1152,1536]{1,0:T(8,128)(2,1)} fusion(bf16[1536,1536]{1,0:T(8,128)(2,1)} %bitcast.138, s32[2048]{0:T(1024)S(1)} %copy-done.34), kind=kCustom, calls=%fused_computation.1 | custom fusion | bytes 7082496 | tf_op jit(solution)/shard_map/gather | solution.py:148
  481.5 6.0 fusion.45
  487.6 8.9 %fusion.23 = bf16[1152,512]{0,1:T(8,128)(2,1)S(1)} fusion(f32[1152,512]{0,1:T(8,128)} %copy-done.7, bf16[2048,512]{1,0:T(8,128)(2,1)} %param.28, f32[1152,2048]{1,0:T(8,128)} %copy-done.59), kind=kOutput, calls=%fused_computation.53 | convolution fusion | flops 2438332416 | bytes 15073280 | tf_op jit(solution)/shard_map/dot_general | solution.py:182
  498.1 5.4 fusion.28
  506.7 41.6 %all-reduce = (f32[512]{0:T(512)}, f32[512]{0:T(512)}, f32[512]{0:T(512)}, f32[512]{0:T(512)}, f32[512]{0:T(512)}) all-reduce(f32[512]{0:T(512)S(1)} %get-tuple-element.164, f32[512]{0:T(512)S(1)} %get-tuple-element.168, f32[512]{0:T(512)S(1)} %copy-done.49, ...), channel_id=1, replica_groups=mesh['dp'=8,'group'=4] {'dp','group'}, use_global_device_ids=true, to_apply=%region_22.23 | all-reduce | flops 2560 | bytes 20480 | tf_op jit(solution)/shard_map/psum | solution.py:220
  548.3 173.4 %all-reduce.4.cloned.1.call-done = (f32[512,1536]{1,0:T(8,128)}, f32[512,512]{1,0:T(8,128)}, f32[512,2048]{1,0:T(8,128)}, f32[2048,512]{1,0:T(8,128)}) async-done(((f32[512,1536]{1,0:T(8,128)}, f32[512,512]{1,0:T(8,128)}, f32[512,2048]{1,0:T(8,128)}, f32[2048,512]{1,0:T(8,128)}), (f32[512,1536]{1,0:T(8,128)}, f32[512,512]{1,0:T(8,128)}, f32[512,2048]{1,0:T(8,128)}, ...) | async-done | bytes 12582928 | tf_op jit(solution)/shard_map/psum | solution.py:220
  721.7 3.9 copy.170
  (257 shorter events, 59.6 us)
Async XLA Ops:
  7.2 199.7 %copy-start = (bf16[512,2048]{1,0:T(8,128)(2,1)S(1)}, bf16[512,2048]{1,0:T(8,128)(2,1)}, u32[]{:S(2)}) copy-start(bf16[512,2048]{1,0:T(8,128)(2,1)} %param.27) | copy-start | bytes 6291460
  7.2 8.8 %copy-start.44 = (f32[512]{0:T(512)S(1)}, f32[512]{0:T(512)}, u32[]{:S(2)}) copy-start(f32[512]{0:T(512)} %param.29) | copy-start | bytes 6148
  9.5 7.4 copy-start.37
  14.2 2.6 copy-start.30
  14.3 3.2 copy-start.50
  14.3 3.2 copy-start.57
  16.0 6.0 copy-start.11
  17.8 4.1 copy-start.42
  39.0 60.6 %all-to-all-start = ((bf16[3,4,128,1536]{3,2,0,1:T(8,128)(2,1)}), bf16[3,4,128,1536]{3,2,0,1:T(8,128)(2,1)}, u32[]{:S(2)}, u32[]{:S(2)}) async-start(bf16[3,4,128,1536]{3,2,0,1:T(8,128)(2,1)} %copy.103), calls=%async_computation | async-start | bytes 9437184 | tf_op jit(solution)/shard_map/all_to_all | solution.py:162
  158.6 15.6 %copy-start.21 = (bf16[1152,512]{1,0:T(8,128)(2,1)S(1)}, bf16[1152,512]{1,0:T(8,128)(2,1)}, u32[]{:S(2)}) copy-start(bf16[1152,512]{1,0:T(8,128)(2,1)} %param.20) | copy-start | bytes 3538948
  158.6 17.0 %copy-start.43 = (s32[1152]{0:T(1024)S(1)}, s32[1152]{0:T(1024)}, u32[]{:S(2)}) copy-start(s32[1152]{0:T(1024)} %copy-done.42) | copy-start | bytes 13828
  158.6 35.5 %all-to-all-start.1 = ((bf16[3,4,128,512]{3,2,0,1:T(8,128)(2,1)}), bf16[3,4,128,512]{3,2,0,1:T(8,128)(2,1)}, u32[]{:S(2)}, u32[]{:S(2)}) async-start(bf16[3,4,128,512]{3,2,0,1:T(8,128)(2,1)} %copy.108), calls=%async_computation.1 | async-start | bytes 3145728 | tf_op jit(solution)/shard_map/all_to_all | solution.py:168
  175.6 27.6 %copy-start.33 = (s32[2048]{0:T(1024)}, s32[2048]{0:T(1024)S(1)}, u32[]{:S(2)}) copy-start(s32[2048]{0:T(1024)S(1)} %pad_clamp_fusion) | copy-start | bytes 24580
  196.7 6.5 copy-start.12
  196.7 6.5 copy-start.38
  196.7 6.5 copy-start.45
  205.5 24.2 %copy-start.28 = (f32[1152]{0:T(1024)}, f32[1152]{0:T(1024)S(1)}, u32[]{:S(2)}) copy-start(f32[1152]{0:T(1024)S(1)} %broadcast_multiply_fusion.4) | copy-start | bytes 13828
  206.9 22.9 %copy-start.35 = (f32[1152]{0:T(1024)}, f32[1152]{0:T(1024)S(1)}, u32[]{:S(2)}) copy-start(f32[1152]{0:T(1024)S(1)} %add_rsqrt_fusion) | copy-start | bytes 13828
  206.9 2.9 copy-start.22
  206.9 2.9 copy-start.53
  209.8 8.3 %copy-start.59 = (f32[1152,2048]{1,0:T(8,128)}, f32[1152,2048]{1,0:T(8,128)S(1)}, u32[]{:S(2)}) copy-start(f32[1152,2048]{1,0:T(8,128)S(1)} %fusion.44) | copy-start | bytes 28311556
  218.1 4.7 copy-start.60
  222.8 7.0 copy-start.17
  225.9 3.9 copy-start.8
  225.9 3.9 copy-start.10
  242.5 24.9 %all-to-all-start.2 = ((bf16[3,4,128,512]{3,2,0,1:T(8,128)(2,1)}), bf16[3,4,128,512]{3,2,0,1:T(8,128)(2,1)}, u32[]{:S(2)}, u32[]{:S(2)}) async-start(bf16[3,4,128,512]{3,2,0,1:T(8,128)(2,1)} %copy.113), calls=%async_computation.2 | async-start | bytes 3145728 | tf_op jit(solution)/shard_map/all_to_all | solution.py:196
  285.6 10.6 %copy-start.4 = (bf16[1,512,512]{1,2,0:T(8,128)(2,1)S(1)}, bf16[1,512,512]{1,2,0:T(8,128)(2,1)}, u32[]{:S(2)}) copy-start(bf16[1,512,512]{1,2,0:T(8,128)(2,1)} %copy.144) | copy-start | bytes 1572868 | tf_op jit(solution)/shard_map/while
  296.2 8.5 %copy-start.2 = (bf16[16,512,512]{1,2,0:T(8,128)(2,1)S(1)}, bf16[16,512,512]{1,2,0:T(8,128)(2,1)}, u32[]{:S(2)}) copy-start(bf16[16,512,512]{1,2,0:T(8,128)(2,1)} %multiply_convert_fusion.5) | copy-start | bytes 25165828 | tf_op jit(solution)/shard_map/while
  310.2 2.8 copy-start.15
  310.2 2.8 copy-start.27
  329.7 10.6 %copy-start.4 = (bf16[1,512,512]{1,2,0:T(8,128)(2,1)S(1)}, bf16[1,512,512]{1,2,0:T(8,128)(2,1)}, u32[]{:S(2)}) copy-start(bf16[1,512,512]{1,2,0:T(8,128)(2,1)} %copy.144) | copy-start | bytes 1572868 | tf_op jit(solution)/shard_map/while
  340.2 8.5 %copy-start.2 = (bf16[16,512,512]{1,2,0:T(8,128)(2,1)S(1)}, bf16[16,512,512]{1,2,0:T(8,128)(2,1)}, u32[]{:S(2)}) copy-start(bf16[16,512,512]{1,2,0:T(8,128)(2,1)} %multiply_convert_fusion.5) | copy-start | bytes 25165828 | tf_op jit(solution)/shard_map/while
  354.3 2.8 copy-start.15
  354.3 2.8 copy-start.27
  361.4 2.4 copy-start.20
  373.8 10.6 %copy-start.4 = (bf16[1,512,512]{1,2,0:T(8,128)(2,1)S(1)}, bf16[1,512,512]{1,2,0:T(8,128)(2,1)}, u32[]{:S(2)}) copy-start(bf16[1,512,512]{1,2,0:T(8,128)(2,1)} %copy.144) | copy-start | bytes 1572868 | tf_op jit(solution)/shard_map/while
  384.4 8.5 %copy-start.2 = (bf16[16,512,512]{1,2,0:T(8,128)(2,1)S(1)}, bf16[16,512,512]{1,2,0:T(8,128)(2,1)}, u32[]{:S(2)}) copy-start(bf16[16,512,512]{1,2,0:T(8,128)(2,1)} %multiply_convert_fusion.5) | copy-start | bytes 25165828 | tf_op jit(solution)/shard_map/while
  398.4 2.8 copy-start.15
  398.4 2.8 copy-start.27
  405.9 5.4 copy-start.16
  405.9 58.9 %all-to-all-start.3 = ((bf16[3,4,128,1536]{3,2,0,1:T(8,128)(2,1)}), bf16[3,4,128,1536]{3,2,0,1:T(8,128)(2,1)}, u32[]{:S(2)}, u32[]{:S(2)}) async-start(bf16[3,4,128,1536]{3,2,0,1:T(8,128)(2,1)} %copy.118), calls=%async_computation.3 | async-start | bytes 9437184 | tf_op jit(solution)/shard_map/all_to_all | solution.py:204
  411.0 4.0 copy-start.29
  411.0 4.0 copy-start.36
  411.0 4.0 copy-start.48
  411.0 4.0 copy-start.56
  411.1 310.6 %all-reduce.4.cloned.1.call-start = ((), (), s32[]{:S(2)}) async-start(), calls=%async_computation.4 | async-start | bytes 25165824 | tf_op jit(solution)/shard_map/psum | solution.py:220
  411.3 3.7 copy-start.9
  411.3 10.9 %slice-start = ((s8[9437184]{0:T(1024)(128)(4,1)}), s8[4194304]{0:T(1024)(128)(4,1)S(1)}, s32[]{:S(2)}) async-start(s8[9437184]{0:T(1024)(128)(4,1)} %bitcast.163), calls=%async_computation.5 | async-start | bytes 8388608
  415.0 7.2 copy-start.23
  415.0 7.2 slice-start.1
  415.0 7.2 slice-start.2
  427.5 42.1 %copy-start.34 = (s32[2048]{0:T(1024)S(1)}, s32[2048]{0:T(1024)}, u32[]{:S(2)}) copy-start(s32[2048]{0:T(1024)} %copy-done.33) | copy-start | bytes 24580
  469.6 11.8 %copy-start.13 = (bf16[1152,512]{0,1:T(8,128)(2,1)S(1)}, bf16[1152,512]{0,1:T(8,128)(2,1)}, u32[]{:S(2)}) copy-start(bf16[1152,512]{0,1:T(8,128)(2,1)} %copy-done.11) | copy-start | bytes 3538948
  469.6 11.8 %copy-start.32 = (f32[1152]{0:T(1024)S(1)}, f32[1152]{0:T(1024)}, u32[]{:S(2)}) copy-start(f32[1152]{0:T(1024)} %copy-done.31) | copy-start | bytes 13828
  469.6 11.8 %copy-start.39 = (pred[1152]{0:T(1024)(128)(4,1)S(1)}, pred[1152]{0:T(1024)(128)(4,1)}, u32[]{:S(2)}) copy-start(pred[1152]{0:T(1024)(128)(4,1)} %copy-done.37) | copy-start | bytes 3460
  469.6 11.8 %copy-start.41 = (f32[1152]{0:T(1024)S(1)}, f32[1152]{0:T(1024)}, u32[]{:S(2)}) copy-start(f32[1152]{0:T(1024)} %copy-done.40) | copy-start | bytes 13828
  469.6 11.8 %copy-start.46 = (f32[512]{0:T(512)S(1)}, f32[512]{0:T(512)}, u32[]{:S(2)}) copy-start(f32[512]{0:T(512)} %param.29) | copy-start | bytes 6148
  469.7 11.8 %copy-start.51 = (f32[512]{0:T(512)S(1)}, f32[512]{0:T(512)}, u32[]{:S(2)}) copy-start(f32[512]{0:T(512)} %param.21) | copy-start | bytes 6148
  469.7 11.8 %copy-start.58 = (f32[512]{0:T(512)S(1)}, f32[512]{0:T(512)}, u32[]{:S(2)}) copy-start(f32[512]{0:T(512)} %param.22) | copy-start | bytes 6148
  498.1 5.5 copy-start.6
  721.7 3.9 copy-start.24
  721.7 4.9 copy-start.19
  726.6 3.7 copy-start.18
  726.6 5.7 copy-start.1
  (21 other events, 32.6 us)
Sparse Core Ops, SparseCore 0:
  487.7 233.9 all-reduce.3
where the time goes:
time: 743 us; the launch traced here: 739 us
  waiting for transfers between devices  249 us (34%)
  matrix products  158 us (21%)
  local copies, waits for them, and re-layouts  133 us (18%)
  blocking collectives  97 us (13%)
  other arithmetic  56.1 us (8%)
  starting transfers between devices  30.6 us (4%)
  between operations  15 us (2%)
    psum x1, waiting for transfers between devices, on_device(): lax.psum((grad_ln1_gain, grad_ln1_bias, grad_w_qkv, grad_w_out, grad_ln2_...  173 us
    all_gather x1, blocking collectives, on_device(): lax.all_gather(band_group, 'group', axis=0, tiled=True)  55.4 us
    dot_general x6, matrix products, score_block(): jnp.einsum('qhd,khd->hqk', queries, key_rows, preferred_element_type=jnp....  42.7 us
    psum x1, blocking collectives, on_device(): lax.psum((grad_ln1_gain, grad_ln1_bias, grad_w_qkv, grad_w_out, grad_ln2_...  41.6 us
    all_to_all x1, waiting for transfers between devices, on_device(): lax.all_to_all(grad_sets.reshape(cubes, groups, capacity, 3 * width), 'gr...  37.3 us
    convert_element_type x3, other arithmetic, attend_back(): grad_scores = (probs * (grad_probs - centred)).astype(jnp.bfloat16)  31.7 us
    dot_general x3, matrix products, attend_back(): jnp.einsum('hqk,qhd->khd', probs.astype(jnp.bfloat16), grad_heads, prefer...  25.5 us
    dot_general x4, matrix products, inner_rows(): lax.dot_general(left, right, (((0,), (0,)), ((), ())), preferred_element_...  22.2 us
  transfers between devices with their start and end apart: 5, of which 4 were waited for; matrix products, arithmetic and copies ran while one was open for 5% of the time, Pallas kernels for 0%

commit v1 on v0

v1 whole, which is shorter than its diff:
```python
import functools
import jax
import jax.numpy as jnp
from jax import lax
from jax.experimental import pallas as pl
from jax.experimental.pallas import tpu as pltpu
from jax.sharding import PartitionSpec as P

HEADS = 16
CUBE_TOK = 1536
EPS = 1e-05
LOG2E = 1.4426950408889634
LN2 = 0.6931471805599453
FLOOR = -1e20
MASKED = -1e30

NN = (((1,), (0,)), ((), ()))
NT = (((1,), (1,)), ((), ()))
TN = (((0,), (0,)), ((), ()))
MESH = pl.DeviceIdType.MESH
BF = jnp.bfloat16
F32 = jnp.float32


def dot(left, right, dims=NN):
    return lax.dot_general(left, right, dims, preferred_element_type=F32)


def norm_stats(values):
    centre = values - jnp.mean(values, axis=-1, keepdims=True)
    spread = jnp.mean(centre * centre, axis=-1, keepdims=True)
    recip = lax.rsqrt(spread + EPS)
    return centre * recip, recip


def norm_back(grad_rows, normal, recip, gain):
    scaled = grad_rows * gain
    return recip * (
        scaled
        - jnp.mean(scaled, axis=-1, keepdims=True)
        - normal * jnp.mean(scaled * normal, axis=-1, keepdims=True)
    )


def onehot(dest_row, slots):
    rows = lax.broadcasted_iota(jnp.int32, (slots, dest_row.shape[1]), 0)
    return jnp.where(rows == dest_row, 1.0, 0.0).astype(BF)


def peer(bits):
    me = lax.axis_index("group")
    for bit in bits:
        me = me + (1 - 2 * (lax.rem(me // bit, 2))) * bit
    return (lax.axis_index("dp"), me)


def copy_to(src, dst, sems, index, device):
    return pltpu.make_async_remote_copy(
        src_ref=src, dst_ref=dst, send_sem=sems[0].at[index], recv_sem=sems[1].at[index],
        device_id=device, device_id_type=MESH,
    )


def greet(devices):
    barrier = pltpu.get_barrier_semaphore()
    for device in devices:
        pl.semaphore_signal(barrier, inc=1, device_id=device, device_id_type=MESH)
    pl.semaphore_wait(barrier, len(devices))


def own_dest(ids, capacity, groups):
    tokens = ids.shape[1]
    upper = (
        lax.broadcasted_iota(jnp.int32, (tokens, tokens), 0)
        < lax.broadcasted_iota(jnp.int32, (tokens, tokens), 1)
    )
    upper = jnp.where(upper, 1.0, 0.0).astype(BF)
    total = jnp.zeros(ids.shape, F32)
    for group in range(groups):
        hit = jnp.where(ids == group, 1.0, 0.0)
        ranks = dot(hit.astype(BF), upper)
        total = total + hit * (ranks + float(group * capacity))
    return total.astype(jnp.int32)


def forward_kernel(
    enc, visible, ids, gain, offset, mask_token, w_qkv,
    att, normed, dest, kv, kaug, qt, ot, lse,
    w_mine, wq_t, qbd, vt, away, sems_in, sems_dest, sems_fwd, sems_att,
):
    cubes, quarter = normed.shape[1], normed.shape[2]
    width = enc.shape[1]
    half = width // 2
    groups = kv.shape[1]
    cap = qt.shape[3] // 2
    slots = groups * cap
    hd = width // HEADS
    pack = 128
    per = pack // hd
    packs = half // pack
    factor = LOG2E * hd ** -0.5
    sibling, across, cross = peer((1,)), peer((2,)), peer((1, 2))
    parity = lax.rem(lax.axis_index("group"), 2)

    greet((sibling, across, cross))

    dest[0] = own_dest(ids[...], cap, groups)
    to_peers = []
    for index, device in enumerate((sibling, across, cross)):
        item = copy_to(dest.at[0], dest.at[index + 1], sems_dest, index, device)
        item.start()
        to_peers.append(item)

    def own_rows(c, _):
        rows = enc[pl.ds(c * quarter, quarter), :].astype(F32)
        shown = visible[pl.ds(c * quarter, quarter), :] == 1
        rows = jnp.where(shown, rows, mask_token[...])
        normal, _ = norm_stats(rows)
        normed[0, c] = (normal * gain[...] + offset[...]).astype(BF)
        copy_to(normed.at[0, c], normed.at[2, c], sems_in, cubes + c, across).start()
        copy_to(normed.at[0, c], normed.at[1, c], sems_in, c, sibling).start()
        return 0

    lax.fori_loop(0, cubes, own_rows, 0)

    for part in range(3):
        start = pl.multiple_of(part * width + parity * half, half)
        w_mine[:, part * half:(part + 1) * half] = w_qkv[:, pl.ds(start, half)]
    wq_t[...] = w_mine[:, :half].T

    one_row = lax.broadcasted_iota(jnp.int32, (16, per * 2 * cap), 0)
    for p in range(packs):
        qbd[p] = jnp.zeros(qbd.shape[1:], BF)
        qbd[p, pack:pack + 16, :] = jnp.where(one_row == 0, 1.0, 0.0).astype(BF)
        vt[p, pack:pack + 16, :] = jnp.ones((16, vt.shape[2]), BF)

    def project(r, c):
        rows = normed[r, c]
        row = dest[r, pl.ds(c, 1), :]
        hot = onehot(row, slots)
        values = dot(rows, w_mine[:, half:]).astype(BF)
        placed = dot(hot, values).astype(BF)
        lane = lax.broadcasted_iota(jnp.int32, (cap, 128), 1)
        place = lax.broadcasted_iota(jnp.int32, (cap, 128), 0)
        for s in range(groups):
            kv[c, s, r * cap:(r + 1) * cap, :] = placed[s * cap:(s + 1) * cap, :]
            inside = jnp.logical_and(row >= s * cap, row < (s + 1) * cap)
            count = jnp.sum(jnp.where(inside, 1, 0), axis=1, keepdims=True)
            bias = jnp.where(place < count, 0.0, MASKED)
            extra = jnp.where(lane == 0, bias, jnp.where(lane < 4, 1.0, 0.0))
            kaug[c, s, r * cap:(r + 1) * cap, :] = extra.astype(BF)
        if r < 2:
            queries = (dot(wq_t[...], rows, NT) * factor).astype(BF)
            spread = dot(queries, hot, NT).astype(BF)
            for s in range(groups):
                qt[c, s, :, r * cap:(r + 1) * cap] = spread[:, s * cap:(s + 1) * cap]

    def near_rows(c, _):
        project(0, c)
        copy_to(normed.at[0, c], normed.at[1, c], sems_in, c, sibling).wait_recv()
        project(1, c)
        return 0

    for item in to_peers:
        item.wait_recv()
    lax.fori_loop(0, cubes, near_rows, 0)

    def attend(c, s):
        for p in range(packs):
            lanes = slice(p * pack, (p + 1) * pack)
            for j in range(per):
                qbd[p, j * hd:(j + 1) * hd, j * 2 * cap:(j + 1) * 2 * cap] = qt[
                    c, s, p * pack + j * hd:p * pack + (j + 1) * hd, :]
            vt[p, :pack, :] = kv[c, s, :, half + p * pack:half + (p + 1) * pack].T
            keys = jnp.concatenate([kv[c, s, :, lanes], kaug[c, s]], axis=1)
            scores = dot(keys, qbd[p])
            top = jnp.maximum(jnp.max(scores, axis=0, keepdims=True), FLOOR)
            probs = jnp.exp2(scores - top).astype(BF)
            mixed = dot(vt[p], probs)
            total = jnp.maximum(mixed[pack:pack + 1, :], 1e-30)
            lse[c, s, p:p + 1, :] = top + jnp.log2(total)
            scale = 1.0 / total
            for j in range(per):
                cols = slice(j * 2 * cap, (j + 1) * 2 * cap)
                ot[c, s, p * pack + j * hd:p * pack + (j + 1) * hd, :] = (
                    mixed[j * hd:(j + 1) * hd, cols] * scale[:, cols]
                ).astype(BF)

    def cube(c, _):
        copy_to(normed.at[0, c], normed.at[2, c], sems_in, cubes + c, across).wait_recv()
        forward = copy_to(normed.at[2, c], normed.at[3, c], sems_fwd, c, sibling)
        forward.start()
        project(2, c)
        forward.wait_recv()
        project(3, c)

        def one(s, _):
            attend(c, s)
            return 0

        lax.fori_loop(0, groups, one, 0)
        for r in (1, 0):
            hot = onehot(dest[r, pl.ds(c, 1), :], slots)
            placed = jnp.concatenate(
                [ot[c, s, :, r * cap:(r + 1) * cap] for s in range(groups)], axis=1)
            rows = dot(placed, hot).astype(BF)
            if r == 1:
                away[c] = rows
                copy_to(away.at[c], att.at[c, pl.ds(pl.multiple_of(parity * half, half), half), :],
                        sems_att, c, sibling).start()
            else:
                att[c, pl.ds(pl.multiple_of(parity * half, half), half), :] = rows
        return 0

    lax.fori_loop(0, cubes, cube, 0)

    def finish(c, _):
        copy_to(away.at[c], att.at[c, pl.ds(pl.multiple_of(parity * half, half), half), :],
                sems_att, c, sibling).wait()
        copy_to(normed.at[0, c], normed.at[2, c], sems_in, cubes + c, across).wait_send()
        copy_to(normed.at[0, c], normed.at[1, c], sems_in, c, sibling).wait_send()
        copy_to(normed.at[2, c], normed.at[3, c], sems_fwd, c, sibling).wait_send()
        return 0

    lax.fori_loop(0, cubes, finish, 0)
    for item in to_peers:
        item.wait_send()


def forward_call(enc, visible, ids, gain, offset, mask_token, w_qkv, cubes, groups):
    tokens, width = enc.shape
    quarter = tokens // cubes
    cap = quarter // 3
    half = width // 2
    packs = half // 128
    wide = (128 // (width // HEADS)) * 2 * cap
    vmem = pl.BlockSpec(memory_space=pltpu.VMEM)
    shape = jax.ShapeDtypeStruct
    dma = pltpu.SemaphoreType.DMA
    return pl.pallas_call(
        forward_kernel,
        out_shape=(
            shape((cubes, width, quarter), BF),
            shape((groups, cubes, quarter, width), BF),
            shape((groups, 8, quarter), jnp.int32),
            shape((cubes, groups, groups * cap, width), BF),
            shape((cubes, groups, groups * cap, 128), BF),
            shape((cubes, groups, half, 2 * cap), BF),
            shape((cubes, groups, half, 2 * cap), BF),
            shape((cubes, groups, 8, wide), F32),
        ),
        in_specs=[vmem] * 7,
        out_specs=(vmem,) * 8,
        scratch_shapes=[
            pltpu.VMEM((width, 3 * half), BF),
            pltpu.VMEM((half, width), BF),
            pltpu.VMEM((packs, 256, wide), BF),
            pltpu.VMEM((packs, 144, groups * cap), BF),
            pltpu.VMEM((cubes, half, quarter), BF),
            (dma((2 * cubes,)), dma((2 * cubes,))),
            (dma((3,)), dma((3,))),
            (dma((cubes,)), dma((cubes,))),
            (dma((cubes,)), dma((cubes,))),
        ],
        compiler_params=pltpu.CompilerParams(
            collective_id=0, has_side_effects=True, vmem_limit_bytes=60 * 2**20),
        name="forward",
    )(enc, visible, ids, gain, offset, mask_token, w_qkv)


def pieces(values):
    high = values.astype(BF)
    rest = values - high.astype(F32)
    mid = rest.astype(BF)
    low = (rest - mid.astype(F32)).astype(BF)
    return high, mid, low


def backward_kernel(
    grad_att, kv, kaug, qt, ot, lse, normed, dest, w_qkv, enc, visible, mask_token, gain, grad_middle,
    grad_enc, grad_qkv, small,
    w_mine, near, dot_slots, qbd, dobd, grad_kv, grad_qt, own_sum, out_sib, in_sib, out_fwd, in_fwd,
    out_across, in_across, sems_near, sems_sib, sems_fwd, sems_across,
):
    cubes, width, quarter = grad_att.shape
    half = width // 2
    groups = kv.shape[1]
    cap = qt.shape[3] // 2
    slots = groups * cap
    hd = width // HEADS
    pack = 128
    per = pack // hd
    packs = half // pack
    factor = hd ** -0.5
    sibling, across = peer((1,)), peer((2,))
    parity = lax.rem(lax.axis_index("group"), 2)
    mine = pl.ds(pl.multiple_of(parity * half, half), half)
    theirs = pl.ds(pl.multiple_of((1 - parity) * half, half), half)

    greet((sibling, across))

    def send_near(c, _):
        copy_to(grad_att.at[c, theirs, :], near.at[c], sems_near, c, sibling).start()
        return 0

    lax.fori_loop(0, cubes, send_near, 0)

    for part in range(3):
        start = pl.multiple_of(part * width + parity * half, half)
        w_mine[:, part * half:(part + 1) * half] = w_qkv[:, pl.ds(start, half)]
    one_row = lax.broadcasted_iota(jnp.int32, (16, per * 2 * cap), 0)
    for p in range(packs):
        qbd[p] = jnp.zeros(qbd.shape[1:], BF)
        dobd[p] = jnp.zeros(dobd.shape[1:], BF)
    grad_qkv[...] = jnp.zeros(grad_qkv.shape, F32)
    small[...] = jnp.zeros(small.shape, F32)

    def extra_rows(first, values):
        high, mid, low = pieces(-values)
        rows = jnp.where(
            one_row == 0, first,
            jnp.where(one_row == 1, high.astype(F32),
                      jnp.where(one_row == 2, mid.astype(F32),
                                jnp.where(one_row == 3, low.astype(F32), 0.0))))
        return rows.astype(BF)

    def attend_back(c, s):
        for p in range(packs):
            lanes = slice(p * pack, (p + 1) * pack)
            deltas = []
            for j in range(per):
                rows = slice(p * pack + j * hd, p * pack + (j + 1) * hd)
                cols = slice(j * 2 * cap, (j + 1) * 2 * cap)
                qbd[p, j * hd:(j + 1) * hd, cols] = qt[c, s, rows, :]
                grads = dot_slots[c, s, rows, :]
                dobd[p, j * hd:(j + 1) * hd, cols] = grads
                deltas.append(jnp.sum(
                    grads.astype(F32) * ot[c, s, rows, :].astype(F32), axis=0, keepdims=True))
            qbd[p, pack:pack + 16, :] = extra_rows(1.0, lse[c, s, p:p + 1, :])
            dobd[p, pack:pack + 16, :] = extra_rows(0.0, jnp.concatenate(deltas, axis=1))
            extra = kaug[c, s]
            keys = kv[c, s, :, lanes]
            values = kv[c, s, :, half + p * pack:half + (p + 1) * pack]
            probs = jnp.exp2(dot(jnp.concatenate([keys, extra], axis=1), qbd[p]))
            centred = dot(jnp.concatenate([values, extra], axis=1), dobd[p])
            grad_scores = (probs * centred).astype(BF)
            grad_kv[s, :, half + p * pack:half + (p + 1) * pack] = dot(
                probs.astype(BF), dobd[p, :pack, :], NT).astype(BF)
            grad_kv[s, :, lanes] = (dot(grad_scores, qbd[p, :pack, :], NT) * LN2).astype(BF)
            mixed = dot(keys.T, grad_scores) * factor
            for j in range(per):
                rows = slice(p * pack + j * hd, p * pack + (j + 1) * hd)
                cols = slice(j * 2 * cap, (j + 1) * 2 * cap)
                grad_qt[s, rows, :] = mixed[j * hd:(j + 1) * hd, cols].astype(BF)

    def back_project(r, c):
        hot = onehot(dest[r, pl.ds(c, 1), :], slots)
        placed = jnp.concatenate(
            [grad_kv[s, r * cap:(r + 1) * cap, :] for s in range(groups)], axis=0)
        grads = dot(hot, placed, TN).astype(BF)
        if r < 2:
            queries = jnp.concatenate(
                [grad_qt[s, :, r * cap:(r + 1) * cap] for s in range(groups)], axis=1)
            queries = dot(queries, hot).T.astype(BF)
            grads = jnp.concatenate([queries, grads], axis=1)
            grad_qkv[...] += dot(normed[r, c], grads, TN)
            return dot(grads, w_mine[...], NT)
        grad_qkv[:, half:] += dot(normed[r, c], grads, TN)
        return dot(grads, w_mine[:, half:], NT)

    def cube(c, _):
        copy_to(grad_att.at[c, theirs, :], near.at[c], sems_near, c, sibling).wait_recv()
        for r in range(2):
            rows = grad_att[c, mine, :] if r == 0 else near[c]
            hot = onehot(dest[r, pl.ds(c, 1), :], slots)
            spread = dot(rows, hot, NT).astype(BF)
            for s in range(groups):
                dot_slots[c, s, :, r * cap:(r + 1) * cap] = spread[:, s * cap:(s + 1) * cap]

        def one(s, _):
            attend_back(c, s)
            return 0

        lax.fori_loop(0, groups, one, 0)
        out_fwd[c] = back_project(3, c).astype(BF)
        forward = copy_to(out_fwd.at[c], in_fwd.at[c], sems_fwd, c, sibling)
        forward.start()
        partial = back_project(2, c)
        forward.wait_recv()
        out_across[c] = (partial + in_fwd[c].astype(F32)).astype(BF)
        copy_to(out_across.at[c], in_across.at[c], sems_across, c, across).start()
        out_sib[c] = back_project(1, c).astype(BF)
        copy_to(out_sib.at[c], in_sib.at[c], sems_sib, c, sibling).start()
        own_sum[c] = back_project(0, c)
        return 0

    lax.fori_loop(0, cubes, cube, 0)

    def last(c, _):
        rows_at = pl.ds(c * quarter, quarter)
        copy_to(out_sib.at[c], in_sib.at[c], sems_sib, c, sibling).wait_recv()
        copy_to(out_across.at[c], in_across.at[c], sems_across, c, across).wait_recv()
        grads = own_sum[c] + in_sib[c].astype(F32) + in_across[c].astype(F32)
        shown = visible[rows_at, :] == 1
        start = jnp.where(shown, enc[rows_at, :].astype(F32), mask_token[...])
        normal, recip = norm_stats(start)
        small[0:1, :] += jnp.sum(grads * normal, axis=0, keepdims=True)
        small[1:2, :] += jnp.sum(grads, axis=0, keepdims=True)
        total = grad_middle[rows_at, :] + norm_back(grads, normal, recip, gain[...])
        grad_enc[rows_at, :] = jnp.where(shown, total, 0.0).astype(BF)
        small[2:3, :] += jnp.sum(jnp.where(shown, 0.0, total), axis=0, keepdims=True)
        copy_to(grad_att.at[c, theirs, :], near.at[c], sems_near, c, sibling).wait_send()
        copy_to(out_fwd.at[c], in_fwd.at[c], sems_fwd, c, sibling).wait_send()
        copy_to(out_sib.at[c], in_sib.at[c], sems_sib, c, sibling).wait_send()
        copy_to(out_across.at[c], in_across.at[c], sems_across, c, across).wait_send()
        return 0

    lax.fori_loop(0, cubes, last, 0)


def backward_call(grad_att, kv, kaug, qt, ot, lse, normed, dest, w_qkv, enc, visible, mask_token, gain, grad_middle):
    cubes, width, quarter = grad_att.shape
    groups = kv.shape[1]
    cap = quarter // 3
    half = width // 2
    packs = half // 128
    wide = (128 // (width // HEADS)) * 2 * cap
    vmem = pl.BlockSpec(memory_space=pltpu.VMEM)
    shape = jax.ShapeDtypeStruct
    dma = pltpu.SemaphoreType.DMA
    block = pltpu.VMEM((cubes, quarter, width), BF)
    pair = (dma((cubes,)), dma((cubes,)))
    return pl.pallas_call(
        backward_kernel,
        out_shape=(
            shape(enc.shape, BF),
            shape((width, 3 * half), F32),
            shape((8, width), F32),
        ),
        in_specs=[vmem] * 14,
        out_specs=(vmem,) * 3,
        scratch_shapes=[
            pltpu.VMEM((width, 3 * half), BF),
            pltpu.VMEM((cubes, half, quarter), BF),
            pltpu.VMEM((cubes, groups, half, 2 * cap), BF),
            pltpu.VMEM((packs, 256, wide), BF),
            pltpu.VMEM((packs, 256, wide), BF),
            pltpu.VMEM((groups, groups * cap, width), BF),
            pltpu.VMEM((groups, half, 2 * cap), BF),
            pltpu.VMEM((cubes, quarter, width), F32),
            block, block, block, block, block, block,
            pair, pair, pair, pair,
        ],
        compiler_params=pltpu.CompilerParams(
            collective_id=1, has_side_effects=True, vmem_limit_bytes=60 * 2**20),
        name="backward",
    )(grad_att, kv, kaug, qt, ot, lse, normed, dest, w_qkv, enc, visible, mask_token, gain, grad_middle)


def on_device(
    enc, visible, band_group, cotangent, ln1_gain, ln1_bias, w_qkv, w_out,
    ln2_gain, ln2_bias, w_up, w_down, mask_token,
):
    groups = lax.axis_size("group")
    tok_dev, width = enc.shape
    half = width // 2
    quarter = CUBE_TOK // groups
    cubes = tok_dev // quarter
    column = visible.reshape(tok_dev, 1)
    ids = jnp.pad(band_group.reshape(cubes, quarter), ((0, 8 - cubes), (0, 0)), constant_values=-1)
    gain1, mask_row = ln1_gain[None, :], mask_token[None, :]
    att, normed, dest, kv, kaug, qt, ot, lse = forward_call(
        enc, column, ids, gain1, ln1_bias[None, :], mask_row, w_qkv, cubes, groups)
    attended = att.transpose(0, 2, 1).reshape(tok_dev, width)
    start_rows = jnp.where(column == 1, enc.astype(F32), mask_row)
    middle = start_rows + dot(attended, w_out)
    normal2, recip2 = norm_stats(middle)
    second = (normal2 * ln2_gain + ln2_bias).astype(BF)
    hidden = dot(second, w_up)
    active_full, gelu_pull = jax.vjp(lambda v: jax.nn.gelu(v, approximate=True), hidden)
    active = active_full.astype(BF)
    out = (middle + dot(active, w_down)).astype(BF)
    grad_w_down = dot(active, cotangent, TN)
    grad_hidden = gelu_pull(dot(cotangent, w_down, NT))[0].astype(BF)
    grad_w_up = dot(second, grad_hidden, TN)
    grad_second = dot(grad_hidden, w_up, NT)
    grad_ln2_gain = jnp.sum(grad_second * normal2, axis=0)
    grad_ln2_bias = jnp.sum(grad_second, axis=0)
    grad_middle = cotangent.astype(F32) + norm_back(grad_second, normal2, recip2, ln2_gain)
    grad_branch = grad_middle.astype(BF)
    grad_w_out = dot(attended, grad_branch, TN)
    grad_attended = dot(w_out, grad_branch, NT).astype(BF)
    grad_att = grad_attended.reshape(width, cubes, quarter).transpose(1, 0, 2)
    grad_enc, grad_qkv, small = backward_call(
        grad_att, kv, kaug, qt, ot, lse, normed, dest, w_qkv, enc, column, mask_row, gain1, grad_middle)
    parity = lax.rem(lax.axis_index("group"), 2)
    mine = grad_qkv.reshape(width, 3, 1, half)
    blank = jnp.zeros_like(mine)
    grad_w_qkv = jnp.where(
        parity == 0, jnp.concatenate([mine, blank], axis=2), jnp.concatenate([blank, mine], axis=2)
    ).reshape(width, 3 * width)
    summed = lax.psum(
        (small[0], small[1], grad_w_qkv, grad_w_out, grad_ln2_gain, grad_ln2_bias, grad_w_up,
         grad_w_down, small[2]), ("dp", "group"))
    return (out, grad_enc) + tuple(summed)


def solution(mesh):
    rows, line = P(("dp", "group"), None), P(("dp", "group"))
    return jax.shard_map(
        on_device, mesh=mesh, in_specs=(rows, line, line, rows) + (P(),) * 9,
        out_specs=(rows, rows) + (P(),) * 9, check_vma=False)
```

time: 743 us -> 428 us (0.58)
  Pallas kernels: 0 us -> 122 us
  matrix products: 158 us -> 38.3 us
  local copies, waits for them, and re-layouts: 133 us -> 24.5 us
  waiting for transfers between devices: 249 us -> 183 us
  blocking collectives: 97 us -> 42.2 us
  other arithmetic: 56.1 us -> 2.77 us
  starting transfers between devices: 30.6 us -> 0.04 us
    pallas_call x0 -> x2, Pallas kernels: none -> 122 us  [the longest x1 71.8 us: backward_call(): pl.pallas_call(backward_kernel, out_shape=(shape(enc.shape, BF), shape((w...]
    dot_general x33 -> x9, matrix products: 158 us -> 38.3 us  [dot(): return lax.dot_general(left, right, dims, preferred_element_type=F32)]
    all_to_all x4 -> x0, waiting for transfers between devices: 75.9 us -> none  [the longest x1 37.3 us: on_device(): lax.all_to_all(grad_sets.reshape(cubes, groups, capacity, 3 * width), 'gr...]
    all_gather x1 -> x0, blocking collectives: 55.4 us -> none  [on_device(): lax.all_gather(band_group, 'group', axis=0, tiled=True)]
    convert_element_type x6 -> x0, other arithmetic: 31.9 us -> none  [the longest x3 31.7 us: attend_back(): grad_scores = (probs * (grad_probs - centred)).astype(jnp.bfloat16)]
    all_to_all x4 -> x0, starting transfers between devices: 30.4 us -> none  [the longest x1 15.6 us: on_device(): lax.all_to_all(owner_attended.reshape(cubes, groups, capacity, width), 'g...]
    scatter x2 -> x0, local copies, waits for them, and re-layouts: 20.7 us -> none  [dispatch(): buffer = jnp.zeros((cubes * groups * capacity, rows.shape[1]), rows.dtype...]
    gather x2 -> x0, local copies, waits for them, and re-layouts: 18.2 us -> none  [collect(): return buffer.reshape(cubes * groups * capacity, -1)[destination]]
  transfers between devices with their start and end apart: 5 -> 1, of which waited for: 4 -> 1; matrix products, arithmetic and copies ran while one was open for 5% -> 2% of each run, Pallas kernels for 0% -> 0%
where the time goes in v1:
time: 428 us; the launch traced here: 427 us
  waiting for transfers between devices  183 us (43%)
  Pallas kernels  122 us (29%)
  blocking collectives  42.2 us (10%)
  matrix products  38.3 us (9%)
  local copies, waits for them, and re-layouts  24.5 us (6%)
  between operations  14.2 us (3%)
    psum x1, waiting for transfers between devices, on_device(): lax.psum((small[0], small[1], grad_w_qkv, grad_w_out, grad_ln2_gain, grad...  182 us
    pallas_call x1, Pallas kernels, backward_call(): pl.pallas_call(backward_kernel, out_shape=(shape(enc.shape, BF), shape((w...  71.8 us
    pallas_call x1, Pallas kernels, forward_call(): pl.pallas_call(forward_kernel, out_shape=(shape((cubes, width, quarter),...  50.5 us
    psum x1, blocking collectives, on_device(): lax.psum((small[0], small[1], grad_w_qkv, grad_w_out, grad_ln2_gain, grad...  42.2 us
    dot_general x9, matrix products, dot(): return lax.dot_general(left, right, dims, preferred_element_type=F32)  38.3 us
    unnamed x41, local copies, waits for them, and re-layouts  12.9 us
  transfers between devices with their start and end apart: 1, of which 1 were waited for; matrix products, arithmetic and copies ran while one was open for 2% of the time, Pallas kernels for 0%

profile of v1, /device:TPU:0, one launch (start us, length us, event | category | flops | bytes accessed | tf_op | source)
XLA Modules:
  0.0 426.8 jit_solution(15683936870125764859)
XLA Ops:
  7.2 0.0 copy-start
  7.2 0.0 all-reduce.7.cloned.1.call-start
  7.2 0.8 broadcast_compare_fusion
  8.1 1.7 reshape.71.visible
  9.8 0.7 reshape.66
  10.5 0.6 pad.6.ids
  11.1 0.0 copy-start.5
  11.1 0.0 copy-start.15
  11.1 50.5 %forward.1 = (bf16[3,512,384]{2,1,0:T(8,128)(2,1)}, bf16[4,3,384,512]{3,2,1,0:T(8,128)(2,1)}, s32[4,8,384]{2,1,0:T(8,128)}, bf16[3,4,512,512]{3,2,1,0:T(8,128)(2...) custom-call(bf16[1152,512]{1,0:T(8,128)(2,1)} %enc.3, ...), custom_call_target="tpu_custom_call" | custom-call | tf_op jit(solution)/shard_map/forward/pallas_call | solution.py:240
  61.6 2.4 copy.33
  64.0 0.0 copy-done.5
  64.0 0.0 copy-done.15
  64.0 2.3 fusion.15
  66.3 0.0 copy-start.2
  66.3 0.0 copy-start.13
  66.3 0.0 copy-start.14
  66.3 0.5 multiply_reduce_fusion.2
  66.8 0.0 copy-done
  66.8 0.2 copy-done.13
  67.0 0.0 copy-done.14
  67.0 0.0 copy-start.8
  67.0 2.7 fusion.12
  69.8 0.0 copy-done.8
  69.8 0.0 copy-start.17
  69.8 0.0 copy-start.16
  69.8 5.2 %fusion.13 = f32[2048,512]{1,0:T(8,128)} fusion(bf16[1152,512]{1,0:T(8,128)(2,1)S(1)} %copy-done.8, f32[1152,2048]{1,0:T(8,128)S(1)} %fusion.12), kind=kOutput, calls=%fused_computation.32 | convolution fusion | flops 2437152768 | bytes 14811136 | tf_op jit(solution)/shard_map/dot_general | solution.py:26
  75.0 0.0 copy-done.17
  75.0 0.0 copy-done.16
  75.0 8.2 %fusion.6 = bf16[1152,2048]{1,0:T(8,128)(2,1)S(1)} fusion(f32[1152,2048]{1,0:T(8,128)S(1)} %fusion.12, bf16[1152,512]{1,0:T(8,128)(2,1)S(1)} %copy-done.8, bf16[2048,512]{1,0:T(8,128)(2,1)S(1)} %copy-done.16), kind=kOutput, calls=%fused_computation.8 | convolution fusion | flops 2463105024 | bytes 17432576 | tf_op jit(solution)/shard_map/dot_general | solution.py:26
  83.2 3.4 multiply_reduce_fusion
  86.7 4.9 %fusion.11 = f32[512,2048]{1,0:T(8,128)} fusion(bf16[1152,2048]{1,0:T(8,128)(2,1)S(1)} %fusion.6, f32[1152,512]{1,0:T(8,128)S(1)} %get-tuple-element.61, f32[512]{0:T(512)S(1)} %copy-done.14, f32[512]{0:T(512)S(1)} %copy-done.13, f32[1152]{0:T(1024)S(1)} %add_rsqrt_fusion, f32[1152]{0:T(1024)S(1)} %broadcast_multiply_fusion.2), kind=kOutput, calls=%fused_computation.30 | convolution fusion | flops 2418868224 | bytes 11285504 | tf_op jit(solution)/shard_map/dot_general | solution.py:26
  91.6 0.0 copy-done.2
  91.6 0.0 copy-start.10
  91.6 1.0 multiply_add_fusion.grad_middle
  92.7 0.2 copy-done.10
  92.9 0.0 copy-start.4
  92.9 0.0 copy-start.12
  92.9 1.9 fusion.8
  94.8 0.0 copy-done.4
  94.8 0.0 copy-done.12
  94.8 0.8 convolution_convert_fusion
  95.6 1.4 copy.35
  97.0 71.8 %backward.1 = (bf16[1152,512]{1,0:T(8,128)(2,1)}, f32[512,768]{1,0:T(8,128)}, f32[8,512]{1,0:T(8,128)}) custom-call(bf16[3,512,384]{2,1,0:T(8,128)(2,1)} %bitcast.29, bf16[3,4,512,512]{3,2,1,0:T(8,128)(2,1)} %get-tuple-element.23.kv, bf16[3,4,512,128]{3,2,1,0:T(8,128)(2,1)} %get-tuple-element.24.kaug, bf16[3,4,256,256]{3,2,1,0:T(8,128)(2,1)} %get-tuple-element.25.qt, ...), custom_call_target="tpu_custom_call" | custom-call | tf_op jit(solution)/shard_map/backward/pallas_call | solution.py:433
  168.8 1.9 copy.37
  170.7 0.4 pad_select_fusion
  171.1 2.0 copy.38
  173.1 0.0 copy-start.3
  173.1 0.0 all-reduce.7.cloned.1.call-update
  173.1 0.9 fusion.14
  174.0 42.2 %all-reduce.3 = (f32[512]{0:T(512)}, f32[512]{0:T(512)}, f32[512]{0:T(512)}, f32[512]{0:T(512)}, f32[512]{0:T(512)}) all-reduce(f32[512]{0:T(512)S(1)} %bitcast.35, f32[512]{0:T(512)S(1)} %bitcast.34, f32[512]{0:T(512)S(1)} %get-tuple-element.44, f32[512]{0:T(512)S(1)} %get-tuple-element.47, ...), channel_id=1, replica_groups=mesh['dp'=8,'group'=4] {'dp','group'}, use_global_device_ids=true, to_apply=%region_4.5 | all-reduce | flops 2560 | bytes 20480 | tf_op jit(solution)/shard_map/psum | solution.py:502
  216.2 0.0 copy-done.3
  216.2 8.9 %fusion.7 = bf16[1152,512]{1,0:T(8,128)(2,1)} fusion(f32[1152,512]{1,0:T(8,128)S(1)} %copy-done.3, bf16[2048,512]{1,0:T(8,128)(2,1)} %param.24, f32[1152,2048]{1,0:T(8,128)} %copy-done.17), kind=kOutput, calls=%fused_computation.13 | convolution fusion | flops 2438332416 | bytes 15073280 | tf_op jit(solution)/shard_map/dot_general | solution.py:26
  225.1 182.5 %all-reduce.7.cloned.1.call-done = (f32[512,1536]{0,1:T(8,128)}, f32[512,512]{1,0:T(8,128)}, f32[512,2048]{1,0:T(8,128)}, f32[2048,512]{1,0:T(8,128)}) async-done(((f32[512,1536]{0,1:T(8,128)}, f32[512,512]{1,0:T(8,128)}, f32[512,2048]{1,0:T(8,128)}, f32[2048,512]{1,0:T(8,128)}), (f32[512,1536]{0,1:T(8,128)}, f32[512,512]{1,0:T(8,128)}, f32[512,2048]{1,0:T(8,128)}, ...) | async-done | bytes 12582928 | tf_op jit(solution)/shard_map/psum | solution.py:502
  407.6 0.0 copy-start.9
  407.6 3.7 copy.39
  411.3 0.0 copy-done.9
  411.3 1.0 copy.46
  412.3 0.0 copy-done.11
  412.3 1.0 copy.47
  413.3 1.0 copy-done.7
  414.3 2.1 copy.48
  416.4 1.6 copy-done.6
  418.0 2.0 copy.49
  420.0 0.0 copy-done.1
  (7 shorter events, 0.0 us)
Async XLA Ops:
  7.2 59.6 %copy-start = (bf16[512,2048]{1,0:T(8,128)(2,1)S(1)}, bf16[512,2048]{1,0:T(8,128)(2,1)}, u32[]{:S(2)}) copy-start(bf16[512,2048]{1,0:T(8,128)(2,1)} %param.23) | copy-start | bytes 6291460
  7.2 400.4 %all-reduce.7.cloned.1.call-start = ((), (), s32[]{:S(2)}) async-start(), calls=%async_computation | async-start | bytes 25165824 | tf_op jit(solution)/shard_map/psum | solution.py:502
  11.1 52.9 %copy-start.5 = (bf16[1152,512]{1,0:T(8,128)(2,1)S(1)}, bf16[1152,512]{1,0:T(8,128)(2,1)}, u32[]{:S(2)}) copy-start(bf16[1152,512]{1,0:T(8,128)(2,1)} %enc.3) | copy-start | bytes 3538948
  11.1 52.9 %copy-start.15 = (f32[512]{0:T(512)S(1)}, f32[512]{0:T(512)}, u32[]{:S(2)}) copy-start(f32[512]{0:T(512)} %param.25) | copy-start | bytes 6148
  66.3 25.3 %copy-start.2 = (f32[1152,512]{1,0:T(8,128)}, f32[1152,512]{1,0:T(8,128)S(1)}, u32[]{:S(2)}) copy-start(f32[1152,512]{1,0:T(8,128)S(1)} %get-tuple-element.61) | copy-start | bytes 7077892
  66.3 0.7 copy-start.13
  66.3 0.7 copy-start.14
  67.0 2.7 copy-start.8
  69.8 5.3 %copy-start.17 = (f32[1152,2048]{1,0:T(8,128)}, f32[1152,2048]{1,0:T(8,128)S(1)}, u32[]{:S(2)}) copy-start(f32[1152,2048]{1,0:T(8,128)S(1)} %fusion.12) | copy-start | bytes 28311556
  69.8 5.3 %copy-start.16 = (bf16[2048,512]{1,0:T(8,128)(2,1)S(1)}, bf16[2048,512]{1,0:T(8,128)(2,1)}, u32[]{:S(2)}) copy-start(bf16[2048,512]{1,0:T(8,128)(2,1)} %param.24) | copy-start | bytes 6291460
  91.6 1.3 copy-start.10
  92.9 1.9 copy-start.4
  92.9 1.9 copy-start.12
  173.1 43.1 %copy-start.3 = (f32[1152,512]{1,0:T(8,128)S(1)}, f32[1152,512]{1,0:T(8,128)}, u32[]{:S(2)}) copy-start(f32[1152,512]{1,0:T(8,128)} %copy-done.2) | copy-start | bytes 7077892
  407.6 3.7 copy-start.9
  407.6 4.7 %copy-start.11 = (f32[512,512]{1,0:T(8,128)S(1)}, f32[512,512]{1,0:T(8,128)}, u32[]{:S(2)}) copy-start(f32[512,512]{1,0:T(8,128)} %get-tuple-element.81) | copy-start | bytes 3145732
  411.3 3.0 copy-start.7
  414.3 3.7 copy-start.6
  414.3 5.7 %copy-start.1 = (bf16[512,2048]{1,0:T(8,128)(2,1)S(1)}, bf16[512,2048]{1,0:T(8,128)(2,1)}, u32[]{:S(2)}) copy-start(bf16[512,2048]{1,0:T(8,128)(2,1)} %param.23) | copy-start | bytes 6291460
Sparse Core Ops, SparseCore 0:
  173.2 234.2 all-reduce.6

commit v2 on v1

--- a/solution.py
+++ b/solution.py
@@ -11,6 +11,8 @@
 EPS = 1e-05
 LOG2E = 1.4426950408889634
 LN2 = 0.6931471805599453
+GELU_A = 0.7978845608028654
+GELU_B = 0.7978845608028654 * 0.044715
 FLOOR = -1e20
 MASKED = -1e30
 
@@ -83,10 +85,206 @@
     return total.astype(jnp.int32)
 
 
+def bits_of(size):
+    return [1 << k for k in range(size.bit_length() - 1)]
+
+
+def bit_value(name):
+    axis, bit = name
+    return lax.rem(lax.axis_index(axis) // bit, 2)
+
+
+def flip(names):
+    place = {axis: lax.axis_index(axis) for axis in ("dp", "group")}
+    for axis, bit in names:
+        place[axis] = place[axis] + (1 - 2 * bit_value((axis, bit))) * bit
+    return (place["dp"], place["group"])
+
+
+class Butterfly:
+    def __init__(self, acc, send, recv, settled, out, sems, names):
+        self.acc, self.send, self.recv, self.settled, self.out = acc, send, recv, settled, out
+        self.sems, self.names = sems, names
+        self.rows = acc.shape[0]
+        self.halvings = halvings_of(self.rows, len(names))
+        self.stages = len(names)
+
+    def start_row(self, k):
+        low = 0
+        for j in range(min(k, self.halvings)):
+            low = low + bit_value(self.names[j]) * (self.rows >> (j + 1))
+        return low
+
+    def span(self, low, count):
+        return pl.ds(pl.multiple_of(low, 16), count)
+
+    def hop(self, k):
+        if k < self.halvings:
+            count = self.rows >> (k + 1)
+            at = self.rows - (self.rows >> k)
+        else:
+            count = self.rows >> self.halvings
+            at = self.rows + (k - self.halvings - 1) * count
+        where = pl.ds(at, count)
+        return copy_to(self.send.at[where], self.recv.at[where], self.sems, k, flip([self.names[k]])), where, count
+
+    def reduce_start(self, k):
+        item, where, count = self.hop(k)
+        low = self.start_row(k)
+        if k < self.halvings:
+            low = low + (1 - bit_value(self.names[k])) * count
+        self.send[where, :] = self.acc[self.span(low, count), :].astype(BF)
+        item.start()
+
+    def reduce_finish(self, k):
+        item, where, count = self.hop(k)
+        item.wait()
+        if k < self.halvings:
+            rows = self.span(self.start_row(k + 1), count)
+            self.acc[rows, :] += self.recv[where, :].astype(F32)
+        else:
+            rows = self.span(self.start_row(k), count)
+            self.acc[rows, :] = self.send[where, :].astype(F32) + self.recv[where, :].astype(F32)
+
+    def own_piece(self):
+        return self.span(self.start_row(self.halvings), self.rows >> self.halvings)
+
+    def keep(self):
+        return pltpu.make_async_copy(
+            self.settled, self.out.at[self.own_piece(), :], self.sems[0].at[self.stages + self.halvings])
+
+    def settle(self):
+        self.settled[...] = self.acc[self.own_piece(), :].astype(BF)
+        self.keep().start()
+
+    def gather(self, k):
+        rows = self.span(self.start_row(k + 1), self.rows >> (k + 1))
+        src = self.settled if k == self.halvings - 1 else self.out.at[rows, :]
+        return copy_to(src, self.out.at[rows, :], self.sems, self.stages + k, flip([self.names[k]]))
+
+
+def halvings_of(rows, stages):
+    count = 0
+    while count < stages and (rows >> (count + 1)) % 16 == 0:
+        count += 1
+    return count
+
+
+def staging_rows(rows, stages):
+    count = halvings_of(rows, stages)
+    return rows + (stages - count - 1) * (rows >> count)
+
+
+def reduce_steps(butterflies):
+    stages = butterflies[0].stages
+
+    def first():
+        for b in butterflies:
+            b.reduce_start(0)
+
+    steps = [first]
+    for k in range(stages):
+        def step(k=k):
+            for b in butterflies:
+                b.reduce_finish(k)
+                if k + 1 < stages:
+                    b.reduce_start(k + 1)
+                else:
+                    b.settle()
+        steps.append(step)
+    return steps
+
+
+def gather_steps(butterflies):
+    halvings = max(b.halvings for b in butterflies)
+
+    def first():
+        for b in butterflies:
+            b.gather(b.halvings - 1).start()
+
+    steps = [first]
+    for k in range(halvings - 1, -1, -1):
+        def step(k=k):
+            for b in butterflies:
+                if k < b.halvings:
+                    b.gather(k).wait()
+                    if k == b.halvings - 1:
+                        b.keep().wait()
+                    if k > 0:
+                        b.gather(k - 1).start()
+        steps.append(step)
+    return steps
+
+
+def joined(before, after):
+    def both():
+        before[-1]()
+        after[0]()
+
+    return before[:-1] + [both] + after[1:]
+
+
+def path_orders(names, count):
+    head, tail = names[:count], names[count:]
+    return [head[k:] + head[:k] + tail for k in range(count)]
+
+
+def chip_bits(n_dp, n_group):
+    return [("group", b) for b in bits_of(n_group) if b > 1] + [("dp", b) for b in bits_of(n_dp)]
+
+
+def lanes_of(p):
+    return slice(p * 128, (p + 1) * 128)
+
+
+PARTS = 4
+
+def small_groups(n_dp, n_group):
+    names = [("group", b) for b in bits_of(n_group)] + [("dp", b) for b in bits_of(n_dp)]
+    groups = [names[:3]]
+    rest = names[3:]
+    while rest:
+        groups.append(rest[:2])
+        rest = rest[2:]
+    return groups
+
+
+class SmallSum:
+    def __init__(self, buf, sems, names):
+        self.buf, self.sems, self.names = buf, sems, names
+        self.count = 1 << len(names)
+
+    def copies(self):
+        place = 0
+        for k, name in enumerate(self.names):
+            place = place + bit_value(name) * (1 << k)
+        items = []
+        for t in range(1, self.count):
+            others = [name for k, name in enumerate(self.names) if (t >> k) & 1]
+            items.append(copy_to(self.buf.at[place], self.buf.at[place], self.sems, t, flip(others)))
+        return place, items
+
+    def start(self, values):
+        place, items = self.copies()
+        self.buf[place] = values
+        for item in items:
+            item.start()
+
+    def finish(self):
+        _, items = self.copies()
+        for item in items:
+            item.wait()
+        total = self.buf[0]
+        for j in range(1, self.count):
+            total = total + self.buf[j]
+        return total
+
+
 def forward_kernel(
     enc, visible, ids, gain, offset, mask_token, w_qkv,
-    att, normed, dest, kv, kaug, qt, ot, lse,
-    w_mine, wq_t, qbd, vt, away, sems_in, sems_dest, sems_fwd, sems_att,
+    att, normed_out, dest, kv_out, kaug_out, qt_out, ot_out, lse,
+    sems_load,
+    normed, kv, kaug, qt, ot, w_mine, wq_t, qbd, vt, away, sems_in, sems_dest, sems_fwd, sems_att, sems_store,
 ):
     cubes, quarter = normed.shape[1], normed.shape[2]
     width = enc.shape[1]
@@ -102,7 +300,14 @@
     sibling, across, cross = peer((1,)), peer((2,)), peer((1, 2))
     parity = lax.rem(lax.axis_index("group"), 2)
 
-    greet((sibling, across, cross))
+    mine = pl.ds(pl.multiple_of(parity * half, half), half)
+
+    loads = [pltpu.make_async_copy(w_qkv.at[:, pl.ds(pl.multiple_of(p * width + parity * half, half), half)],
+                                   w_mine.at[:, p * half:(p + 1) * half], sems_load.at[p]) for p in range(3)]
+    for item in loads:
+        item.start()
+
+    greet([sibling, across, cross])
 
     dest[0] = own_dest(ids[...], cap, groups)
     to_peers = []
@@ -111,11 +316,13 @@
         item.start()
         to_peers.append(item)
 
-    def own_rows(c, _):
+    def start_rows(c):
         rows = enc[pl.ds(c * quarter, quarter), :].astype(F32)
         shown = visible[pl.ds(c * quarter, quarter), :] == 1
-        rows = jnp.where(shown, rows, mask_token[...])
-        normal, _ = norm_stats(rows)
+        return jnp.where(shown, rows, mask_token[...])
+
+    def own_rows(c, _):
+        normal, _ = norm_stats(start_rows(c))
         normed[0, c] = (normal * gain[...] + offset[...]).astype(BF)
         copy_to(normed.at[0, c], normed.at[2, c], sems_in, cubes + c, across).start()
         copy_to(normed.at[0, c], normed.at[1, c], sems_in, c, sibling).start()
@@ -123,9 +330,8 @@
 
     lax.fori_loop(0, cubes, own_rows, 0)
 
-    for part in range(3):
-        start = pl.multiple_of(part * width + parity * half, half)
-        w_mine[:, part * half:(part + 1) * half] = w_qkv[:, pl.ds(start, half)]
+    for item in loads:
+        item.wait()
     wq_t[...] = w_mine[:, :half].T
 
     one_row = lax.broadcasted_iota(jnp.int32, (16, per * 2 * cap), 0)
@@ -186,6 +392,14 @@
                     mixed[j * hd:(j + 1) * hd, cols] * scale[:, cols]
                 ).astype(BF)
 
+    def stores(c):
+        pairs = [(ot.at[c], ot_out.at[c]), (kv.at[c], kv_out.at[c]), (kaug.at[c], kaug_out.at[c]),
+                 (qt.at[c], qt_out.at[c]), (normed.at[:, c], normed_out.at[:, c])]
+        return [pltpu.make_async_copy(src, dst, sems_store.at[c, k]) for k, (src, dst) in enumerate(pairs)]
+
+    def attended_copy(c):
+        return copy_to(away.at[c], att.at[c, mine, :], sems_att, c, sibling)
+
     def cube(c, _):
         copy_to(normed.at[0, c], normed.at[2, c], sems_in, cubes + c, across).wait_recv()
         forward = copy_to(normed.at[2, c], normed.at[3, c], sems_fwd, c, sibling)
@@ -193,6 +407,8 @@
         project(2, c)
         forward.wait_recv()
         project(3, c)
+        for item in stores(c)[1:]:
+            item.start()
 
         def one(s, _):
             attend(c, s)
@@ -206,17 +422,18 @@
             rows = dot(placed, hot).astype(BF)
             if r == 1:
                 away[c] = rows
-                copy_to(away.at[c], att.at[c, pl.ds(pl.multiple_of(parity * half, half), half), :],
-                        sems_att, c, sibling).start()
+                attended_copy(c).start()
             else:
-                att[c, pl.ds(pl.multiple_of(parity * half, half), half), :] = rows
+                att[c, mine, :] = rows
+        stores(c)[0].start()
         return 0
 
     lax.fori_loop(0, cubes, cube, 0)
 
     def finish(c, _):
-        copy_to(away.at[c], att.at[c, pl.ds(pl.multiple_of(parity * half, half), half), :],
-                sems_att, c, sibling).wait()
+        for item in stores(c):
+            item.wait()
+        attended_copy(c).wait()
         copy_to(normed.at[0, c], normed.at[2, c], sems_in, cubes + c, across).wait_send()
         copy_to(normed.at[0, c], normed.at[1, c], sems_in, c, sibling).wait_send()
         copy_to(normed.at[2, c], normed.at[3, c], sems_fwd, c, sibling).wait_send()
@@ -235,6 +452,7 @@
     packs = half // 128
     wide = (128 // (width // HEADS)) * 2 * cap
     vmem = pl.BlockSpec(memory_space=pltpu.VMEM)
+    far = pl.BlockSpec(memory_space=pl.ANY)
     shape = jax.ShapeDtypeStruct
     dma = pltpu.SemaphoreType.DMA
     return pl.pallas_call(
@@ -249,9 +467,15 @@
             shape((cubes, groups, half, 2 * cap), BF),
             shape((cubes, groups, 8, wide), F32),
         ),
-        in_specs=[vmem] * 7,
-        out_specs=(vmem,) * 8,
+        in_specs=[vmem] * 6 + [far],
+        out_specs=(vmem, far, vmem, far, far, far, far, vmem),
         scratch_shapes=[
+            dma((3,)),
+            pltpu.VMEM((groups, cubes, quarter, width), BF),
+            pltpu.VMEM((cubes, groups, groups * cap, width), BF),
+            pltpu.VMEM((cubes, groups, groups * cap, 128), BF),
+            pltpu.VMEM((cubes, groups, half, 2 * cap), BF),
+            pltpu.VMEM((cubes, groups, half, 2 * cap), BF),
             pltpu.VMEM((width, 3 * half), BF),
             pltpu.VMEM((half, width), BF),
             pltpu.VMEM((packs, 256, wide), BF),
@@ -261,6 +485,7 @@
             (dma((3,)), dma((3,))),
             (dma((cubes,)), dma((cubes,))),
             (dma((cubes,)), dma((cubes,))),
+            dma((cubes, 5)),
         ],
         compiler_params=pltpu.CompilerParams(
             collective_id=0, has_side_effects=True, vmem_limit_bytes=60 * 2**20),
@@ -276,16 +501,22 @@
     return high, mid, low
 
 
-def backward_kernel(
-    grad_att, kv, kaug, qt, ot, lse, normed, dest, w_qkv, enc, visible, mask_token, gain, grad_middle,
-    grad_enc, grad_qkv, small,
-    w_mine, near, dot_slots, qbd, dobd, grad_kv, grad_qt, own_sum, out_sib, in_sib, out_fwd, in_fwd,
-    out_across, in_across, sems_near, sems_sib, sems_fwd, sems_across,
+def layer_kernel(
+    n_dp, n_group,
+    att_in, kv_in, kaug_in, qt_in, ot_in, lse, normed_in, dest, w_qkv, enc, visible, mask_token, gain,
+    cot_in, w_out_in, w_up_in, w_down_in, gain2, offset2,
+    out, grad_enc, sum_ffn, sum_qkv, sum_small,
+    kv_at, kaug_at, qt_at, ot_at, normed_at, grads_at, turn, sems_read, sems_turn,
+    cot, w_out, w_up, w_down, att, middle, second, backs, result, grads_sum, spare, w_mine, sems_load, sems_out,
+    acc, give, pair, recv, settled, sems_core, sems_ffn,
+    grad_qkv, small, send_qkv, recv_qkv, settled_qkv, small_bufs, sems_qkv, sems_pair, sems_small,
+    dot_slots, qbd, dobd, grad_qt, in_sib, in_fwd, in_across, sems_sib, sems_fwd, sems_across,
 ):
-    cubes, width, quarter = grad_att.shape
+    cubes, quarter, width = middle.shape
     half = width // 2
-    groups = kv.shape[1]
-    cap = qt.shape[3] // 2
+    blocks = w_up.shape[0]
+    groups = kv_at.shape[1]
+    cap = qt_at.shape[3] // 2
     slots = groups * cap
     hd = width // HEADS
     pack = 128
@@ -296,24 +527,210 @@
     parity = lax.rem(lax.axis_index("group"), 2)
     mine = pl.ds(pl.multiple_of(parity * half, half), half)
     theirs = pl.ds(pl.multiple_of((1 - parity) * half, half), half)
-
-    greet((sibling, across))
-
-    def send_near(c, _):
-        copy_to(grad_att.at[c, theirs, :], near.at[c], sems_near, c, sibling).start()
-        return 0
-
-    lax.fori_loop(0, cubes, send_near, 0)
-
-    for part in range(3):
-        start = pl.multiple_of(part * width + parity * half, half)
-        w_mine[:, part * half:(part + 1) * half] = w_qkv[:, pl.ds(start, half)]
+    grad_kv, own_sum, out_fwd, out_sib, out_across = w_up, result, cot, second, backs
+
+    core = ("group", 1)
+    others = chip_bits(n_dp, n_group)
+    paths = path_orders(others, PARTS)
+    qkv = [
+        Butterfly(grad_qkv.at[p], send_qkv.at[p], recv_qkv.at[p], settled_qkv.at[p], sum_qkv.at[parity, p],
+                  (sems_qkv[0].at[p], sems_qkv[1].at[p]), order)
+        for p, order in enumerate(path_orders(others, 3))]
+    qkv_steps = joined(reduce_steps(qkv), gather_steps(qkv))
+    smalls = [
+        SmallSum(small_bufs[k], (sems_small[0].at[k], sems_small[1].at[k]), names)
+        for k, names in enumerate(small_groups(n_dp, n_group))]
+
+    def place_of(j, side):
+        if j < blocks:
+            return sum_ffn.at[j + side * blocks]
+        return sum_ffn.at[2 * blocks, pl.ds(pl.multiple_of(side * half, half), half)]
+
+    def rows_in(j):
+        return width if j < blocks else half
+
+    def butterflies(j):
+        count = rows_in(j)
+        return [
+            Butterfly(acc.at[j, :count, lanes_of(p)], give.at[j, :, lanes_of(p)], recv.at[j, :, lanes_of(p)],
+                      settled.at[j, :count >> halvings_of(count, len(others)), lanes_of(p)],
+                      place_of(j, parity).at[:, lanes_of(p)],
+                      (sems_ffn[0].at[j, p], sems_ffn[1].at[j, p]), paths[p]) for p in range(PARTS)]
+
+    def summing(j):
+        count = rows_in(j)
+        inner = reduce_steps(butterflies(j))
+        exchange = copy_to(give.at[j, :count], pair.at[j, :count], sems_core, j, sibling)
+
+        def second_step():
+            exchange.wait()
+            acc[j, :count] += pair[j, :count].astype(F32)
+            inner[0]()
+
+        return [exchange.start, second_step] + inner[1:]
+
+    def spreading(sets):
+        steps = gather_steps([b for j in sets for b in butterflies(j)])
+
+        def exchanges():
+            return [
+                copy_to(place_of(j, parity), place_of(j, parity), sems_core, blocks + 1 + j, sibling) for j in sets]
+
+        def last_but_one():
+            steps[-1]()
+            for item in exchanges():
+                item.start()
+
+        def final():
+            for item in exchanges():
+                item.wait()
+
+        return steps[:-1] + [last_but_one, final]
+
+    def reads(c):
+        k = lax.rem(c, 2)
+        pairs = [(kv_in.at[c], kv_at.at[k]), (kaug_in.at[c], kaug_at.at[k]), (qt_in.at[c], qt_at.at[k]),
+                 (ot_in.at[c], ot_at.at[k]), (normed_in.at[:, c], normed_at.at[k])]
+        return [pltpu.make_async_copy(src, dst, sems_read.at[k, n]) for n, (src, dst) in enumerate(pairs)]
+
+    loads = [(w_out_in, w_out), (att_in, att)]
+    loads += [(w_up_in.at[:, j * width:(j + 1) * width], w_up.at[j]) for j in range(blocks)]
+    loads += [(w_down_in.at[j * width:(j + 1) * width, :], w_down.at[j]) for j in range(blocks)]
+    loads += [(cot_in.at[c * quarter:(c + 1) * quarter, :], cot.at[c]) for c in range(cubes)]
+    loads += [(w_qkv.at[:, pl.ds(pl.multiple_of(p * width + parity * half, half), half)],
+               w_mine.at[:, p * half:(p + 1) * half]) for p in range(3)]
+    loads = [pltpu.make_async_copy(src, dst, sems_load.at[k]) for k, (src, dst) in enumerate(loads)]
+    for item in loads:
+        item.start()
+    for c in range(min(2, cubes)):
+        for item in reads(c):
+            item.start()
+
+    meets = {}
+    for names in small_groups(n_dp, n_group):
+        for t in range(1, 1 << len(names)):
+            chosen = [name for k, name in enumerate(names) if (t >> k) & 1]
+            meets[tuple(chosen)] = flip(chosen)
+    for name in [core] + others:
+        meets[(name,)] = flip([name])
+    greet(list(meets.values()))
+
     one_row = lax.broadcasted_iota(jnp.int32, (16, per * 2 * cap), 0)
     for p in range(packs):
         qbd[p] = jnp.zeros(qbd.shape[1:], BF)
         dobd[p] = jnp.zeros(dobd.shape[1:], BF)
     grad_qkv[...] = jnp.zeros(grad_qkv.shape, F32)
     small[...] = jnp.zeros(small.shape, F32)
+
+    def rows_of(c):
+        return pl.ds(c * quarter, quarter)
+
+    def start_rows(c):
+        shown = visible[rows_of(c), :] == 1
+        return shown, jnp.where(shown, enc[rows_of(c), :].astype(F32), mask_token[...])
+
+    def turn_copy(c):
+        return copy_to(turn.at[c], grads_at.at[c, 1], sems_turn, c, sibling)
+
+    def out_copy(c):
+        return pltpu.make_async_copy(second.at[c], out.at[rows_of(c), :], sems_out.at[0, c])
+
+    def enc_copy(c):
+        return pltpu.make_async_copy(second.at[c], grad_enc.at[rows_of(c), :], sems_out.at[1, c])
+
+    def enter(c, _):
+        value = start_rows(c)[1] + dot(att[c], w_out[...], TN)
+        middle[c] = value
+        normal, _ = norm_stats(value)
+        second[c] = (normal * gain2[...] + offset2[...]).astype(BF)
+        return 0
+
+    def block(j, c):
+        rows, cotan = second[c], cot[c]
+        hidden = dot(rows, w_up[j])
+        square = hidden * hidden
+        tanh = jnp.tanh(hidden * (GELU_A + GELU_B * square))
+        slope = 0.5 * (1.0 + tanh)
+        active = (hidden * slope).astype(BF)
+        slope = slope + 0.5 * hidden * (1.0 - tanh * tanh) * (GELU_A + 3.0 * GELU_B * square)
+        grad_hidden = (dot(cotan, w_down[j], NT) * slope).astype(BF)
+        grad_up = dot(rows, grad_hidden, TN)
+        grad_down = dot(active, cotan, TN)
+        kept = jnp.where(parity == 0, grad_up, grad_down)
+        given = jnp.where(parity == 0, grad_down, grad_up)
+        outcome = dot(active, w_down[j])
+        grads = dot(grad_hidden, w_up[j], NT)
+        result[c] = outcome + jnp.where(j > 0, result[c], 0.0)
+        grads_sum[c] = grads + jnp.where(j > 0, grads_sum[c], 0.0)
+        acc[j] = kept + jnp.where(c > 0, acc[j], 0.0)
+        spare[...] = given + jnp.where(c > 0, spare[...], 0.0)
+
+        def hand_over():
+            give[j, :width] = spare[...].astype(BF)
+
+        pl.when(c == cubes - 1)(hand_over)
+
+    def leave(c):
+        second[c] = (middle[c] + result[c]).astype(BF)
+        out_copy(c).start()
+        normal, recip = norm_stats(middle[c])
+        grads = grads_sum[c]
+        small[3:4, :] += jnp.sum(grads * normal, axis=0, keepdims=True)
+        small[4:5, :] += jnp.sum(grads, axis=0, keepdims=True)
+        total = cot[c].astype(F32) + norm_back(grads, normal, recip, gain2[...])
+        middle[c] = total
+        branch = total.astype(BF)
+        back = dot(w_out[...], branch, NT).astype(BF)
+        backs[c] = branch
+        turn[c] = jnp.where(parity == 0, back[half:], back[:half])
+        grads_at[c, 0] = jnp.where(parity == 0, back[:half], back[half:])
+        turn_copy(c).start()
+
+    def out_weights():
+        total = dot(att[0], backs[0])
+        for c in range(1, cubes):
+            total += dot(att[c], backs[c])
+        acc[blocks, :half] = jnp.where(parity == 0, total[:half], total[half:])
+        give[blocks, :half] = jnp.where(parity == 0, total[half:], total[:half]).astype(BF)
+
+    firsts = [summing(j) for j in range(blocks + 1)]
+    seconds = [spreading(sets) for sets in SPREADS]
+    plan = []
+    for number, (steps, places) in enumerate(zip(firsts + seconds, SUM_AT + SPREAD_AT)):
+        if len(places) != len(steps):
+            places = [places[0] + 2 * k for k in range(len(steps))]
+        stage = 0 if number < len(firsts) else len(steps)
+        plan += [(place, stage + k, number, step) for k, (place, step) in enumerate(zip(places, steps))]
+    plan = [(entry[0], entry[-1]) for entry in sorted(plan, key=lambda entry: entry[:3])]
+    lead = blocks * cubes + cubes + 1
+
+    def advance(place):
+        for at, step in plan:
+            if at == place:
+                step()
+
+    for item in loads:
+        item.wait()
+    lax.fori_loop(0, cubes, enter, 0)
+    place = blocks * cubes
+
+    def blocks_step(u, _):
+        block(u // cubes, lax.rem(u, cubes))
+        for at, step in plan:
+            if at <= place:
+                pl.when(u == at - 1)(step)
+        return 0
+
+    lax.fori_loop(0, place, blocks_step, 0)
+    for c in range(cubes):
+        leave(c)
+        place += 1
+        advance(place)
+    out_weights()
+    place += 1
+    advance(place)
+    for c in range(cubes):
+        out_copy(c).wait()
 
     def extra_rows(first, values):
         high, mid, low = pieces(-values)
@@ -325,22 +742,23 @@
         return rows.astype(BF)
 
     def attend_back(c, s):
+        slot = lax.rem(c, 2)
         for p in range(packs):
             lanes = slice(p * pack, (p + 1) * pack)
             deltas = []
             for j in range(per):
                 rows = slice(p * pack + j * hd, p * pack + (j + 1) * hd)
                 cols = slice(j * 2 * cap, (j + 1) * 2 * cap)
-                qbd[p, j * hd:(j + 1) * hd, cols] = qt[c, s, rows, :]
-                grads = dot_slots[c, s, rows, :]
+                qbd[p, j * hd:(j + 1) * hd, cols] = qt_at[slot, s, rows, :]
+                grads = dot_slots[s, rows, :]
                 dobd[p, j * hd:(j + 1) * hd, cols] = grads
                 deltas.append(jnp.sum(
-                    grads.astype(F32) * ot[c, s, rows, :].astype(F32), axis=0, keepdims=True))
+                    grads.astype(F32) * ot_at[slot, s, rows, :].astype(F32), axis=0, keepdims=True))
             qbd[p, pack:pack + 16, :] = extra_rows(1.0, lse[c, s, p:p + 1, :])
             dobd[p, pack:pack + 16, :] = extra_rows(0.0, jnp.concatenate(deltas, axis=1))
-            extra = kaug[c, s]
-            keys = kv[c, s, :, lanes]
-            values = kv[c, s, :, half + p * pack:half + (p + 1) * pack]
+            extra = kaug_at[slot, s]
+            keys = kv_at[slot, s, :, lanes]
+            values = kv_at[slot, s, :, half + p * pack:half + (p + 1) * pack]
             probs = jnp.exp2(dot(jnp.concatenate([keys, extra], axis=1), qbd[p]))
             centred = dot(jnp.concatenate([values, extra], axis=1), dobd[p])
             grad_scores = (probs * centred).astype(BF)
@@ -363,98 +781,255 @@
                 [grad_qt[s, :, r * cap:(r + 1) * cap] for s in range(groups)], axis=1)
             queries = dot(queries, hot).T.astype(BF)
             grads = jnp.concatenate([queries, grads], axis=1)
-            grad_qkv[...] += dot(normed[r, c], grads, TN)
+            weight = dot(normed_at[lax.rem(c, 2), r], grads, TN)
+            for k in range(3):
+                grad_qkv[k] += weight[:, k * half:(k + 1) * half]
             return dot(grads, w_mine[...], NT)
-        grad_qkv[:, half:] += dot(normed[r, c], grads, TN)
+        weight = dot(normed_at[lax.rem(c, 2), r], grads, TN)
+        for k in range(2):
+            grad_qkv[k + 1] += weight[:, k * half:(k + 1) * half]
         return dot(grads, w_mine[:, half:], NT)
 
-    def cube(c, _):
-        copy_to(grad_att.at[c, theirs, :], near.at[c], sems_near, c, sibling).wait_recv()
+    def prepare(c):
+        for item in reads(c):
+            item.wait()
         for r in range(2):
-            rows = grad_att[c, mine, :] if r == 0 else near[c]
+            rows = grads_at[c, r]
             hot = onehot(dest[r, pl.ds(c, 1), :], slots)
             spread = dot(rows, hot, NT).astype(BF)
             for s in range(groups):
-                dot_slots[c, s, :, r * cap:(r + 1) * cap] = spread[:, s * cap:(s + 1) * cap]
+                dot_slots[s, :, r * cap:(r + 1) * cap] = spread[:, s * cap:(s + 1) * cap]
+
+    def cube(c, _):
+        def point(i):
+            for at, step in plan:
+                if at > lead and (at - lead - 1) % POINTS == i and (at - lead - 1) // POINTS < cubes:
+                    pl.when(c == (at - lead - 1) // POINTS)(step)
+
+        turn_copy(c).wait()
+        prepare(c)
+        point(0)
 
         def one(s, _):
             attend_back(c, s)
+            for i in range(groups):
+                pl.when(s == i)(functools.partial(point, i + 1))
             return 0
 
         lax.fori_loop(0, groups, one, 0)
         out_fwd[c] = back_project(3, c).astype(BF)
         forward = copy_to(out_fwd.at[c], in_fwd.at[c], sems_fwd, c, sibling)
         forward.start()
+        point(5)
         partial = back_project(2, c)
         forward.wait_recv()
         out_across[c] = (partial + in_fwd[c].astype(F32)).astype(BF)
         copy_to(out_across.at[c], in_across.at[c], sems_across, c, across).start()
+        point(6)
         out_sib[c] = back_project(1, c).astype(BF)
         copy_to(out_sib.at[c], in_sib.at[c], sems_sib, c, sibling).start()
+        point(7)
         own_sum[c] = back_project(0, c)
+
+        def more():
+            for item in reads(c + 2):
+                item.start()
+
+        pl.when(c + 2 < cubes)(more)
+        point(8)
         return 0
 
     lax.fori_loop(0, cubes, cube, 0)
-
-    def last(c, _):
-        rows_at = pl.ds(c * quarter, quarter)
-        copy_to(out_sib.at[c], in_sib.at[c], sems_sib, c, sibling).wait_recv()
-        copy_to(out_across.at[c], in_across.at[c], sems_across, c, across).wait_recv()
+    qkv_steps[0]()
+    tail = [(at - lead - POINTS * cubes, step) for at, step in plan if at > lead + POINTS * cubes]
+
+    def last(c):
+        copy_to(out_sib.at[c], in_sib.at[c], sems_sib, c, sibling).wait()
+        copy_to(out_across.at[c], in_across.at[c], sems_across, c, across).wait()
+        copy_to(out_fwd.at[c], in_fwd.at[c], sems_fwd, c, sibling).wait_send()
         grads = own_sum[c] + in_sib[c].astype(F32) + in_across[c].astype(F32)
-        shown = visible[rows_at, :] == 1
-        start = jnp.where(shown, enc[rows_at, :].astype(F32), mask_token[...])
+        shown, start = start_rows(c)
         normal, recip = norm_stats(start)
         small[0:1, :] += jnp.sum(grads * normal, axis=0, keepdims=True)
         small[1:2, :] += jnp.sum(grads, axis=0, keepdims=True)
-        total = grad_middle[rows_at, :] + norm_back(grads, normal, recip, gain[...])
-        grad_enc[rows_at, :] = jnp.where(shown, total, 0.0).astype(BF)
+        total = middle[c] + norm_back(grads, normal, recip, gain[...])
+        second[c] = jnp.where(shown, total, 0.0).astype(BF)
+        enc_copy(c).start()
         small[2:3, :] += jnp.sum(jnp.where(shown, 0.0, total), axis=0, keepdims=True)
-        copy_to(grad_att.at[c, theirs, :], near.at[c], sems_near, c, sibling).wait_send()
-        copy_to(out_fwd.at[c], in_fwd.at[c], sems_fwd, c, sibling).wait_send()
-        copy_to(out_sib.at[c], in_sib.at[c], sems_sib, c, sibling).wait_send()
-        copy_to(out_across.at[c], in_across.at[c], sems_across, c, across).wait_send()
-        return 0
-
-    lax.fori_loop(0, cubes, last, 0)
-
-
-def backward_call(grad_att, kv, kaug, qt, ot, lse, normed, dest, w_qkv, enc, visible, mask_token, gain, grad_middle):
-    cubes, width, quarter = grad_att.shape
+
+    fill = list(range(cubes))
+    for k in range(1, len(qkv_steps)):
+        if fill:
+            last(fill.pop(0))
+            if not fill:
+                smalls[0].start(small[...])
+        qkv_steps[k]()
+        while tail and tail[0][0] <= k:
+            tail.pop(0)[1]()
+    pair_qkv = copy_to(sum_qkv.at[parity], sum_qkv.at[parity], sems_pair, 0, sibling)
+    pair_qkv.start()
+    for _, step in tail:
+        step()
+    for k, item in enumerate(smalls):
+        total = item.finish()
+        if k + 1 < len(smalls):
+            smalls[k + 1].start(total)
+    sum_small[...] = total
+    for c in range(cubes):
+        enc_copy(c).wait()
+    pair_qkv.wait()
+
+
+POINTS = 9
+PARTS = 4
+SUM_AT = [
+    [3, 5, 9, 12, 16, 19],
+    [6, 8, 12, 16, 19, 21],
+    [9, 11, 15, 19, 22, 25],
+    [12, 14, 18, 20, 22, 25],
+    [16, 18, 21, 25, 28, 32],
+]
+SPREADS = [[0], [1], [2], [3], [4]]
+SPREAD_AT = [
+    [19, 21, 24, 27, 30, 32],
+    [21, 24, 27, 31, 35, 37],
+    [25, 28, 31, 36, 39, 41],
+    [25, 28, 32, 37, 41, 43],
+    [32, 37, 41, 44, 46, 47],
+]
+
+
+def layer_call(
+    att, kv, kaug, qt, ot, lse, normed, dest, w_qkv, enc, visible, mask_token, gain,
+    cot, w_out, w_up, w_down, gain2, offset2, n_dp, n_group,
+):
+    cubes, width, quarter = att.shape
     groups = kv.shape[1]
     cap = quarter // 3
     half = width // 2
     packs = half // 128
     wide = (128 // (width // HEADS)) * 2 * cap
+    blocks = w_up.shape[1] // width
     vmem = pl.BlockSpec(memory_space=pltpu.VMEM)
+    far = pl.BlockSpec(memory_space=pl.ANY)
     shape = jax.ShapeDtypeStruct
     dma = pltpu.SemaphoreType.DMA
-    block = pltpu.VMEM((cubes, quarter, width), BF)
+    rows = pltpu.VMEM((cubes, quarter, width), BF)
+    sums = pltpu.VMEM((cubes, quarter, width), F32)
+    squares = pltpu.VMEM((blocks, width, width), BF)
     pair = (dma((cubes,)), dma((cubes,)))
+    stages = len(chip_bits(n_dp, n_group))
+    staging = staging_rows(width, stages)
+    kept = max(width >> halvings_of(width, stages), half >> halvings_of(half, stages))
+    kept_qkv = width >> halvings_of(width, stages)
+    small = small_groups(n_dp, n_group)
     return pl.pallas_call(
-        backward_kernel,
+        functools.partial(layer_kernel, n_dp, n_group),
         out_shape=(
             shape(enc.shape, BF),
-            shape((width, 3 * half), F32),
+            shape(enc.shape, BF),
+            shape((2 * blocks + 1, width, width), BF),
+            shape((2, 3, width, half), BF),
             shape((8, width), F32),
         ),
-        in_specs=[vmem] * 14,
-        out_specs=(vmem,) * 3,
+        in_specs=[far] * 5 + [vmem, far, vmem, far] + [vmem] * 4 + [far] * 4 + [vmem] * 2,
+        out_specs=(far, far, far, far, vmem),
         scratch_shapes=[
+            pltpu.VMEM((2,) + kv.shape[1:], BF),
+            pltpu.VMEM((2,) + kaug.shape[1:], BF),
+            pltpu.VMEM((2,) + qt.shape[1:], BF),
+            pltpu.VMEM((2,) + ot.shape[1:], BF),
+            pltpu.VMEM((2, groups, quarter, width), BF),
+            pltpu.VMEM((cubes, 2, half, quarter), BF),
+            pltpu.VMEM((cubes, half, quarter), BF),
+            dma((2, 5)),
+            pair,
+            rows,
+            pltpu.VMEM(w_out.shape, BF),
+            squares,
+            squares,
+            pltpu.VMEM(att.shape, BF),
+            sums,
+            rows,
+            rows,
+            sums,
+            sums,
+            pltpu.VMEM((width, width), F32),
             pltpu.VMEM((width, 3 * half), BF),
-            pltpu.VMEM((cubes, half, quarter), BF),
-            pltpu.VMEM((cubes, groups, half, 2 * cap), BF),
+            dma((2 + 2 * blocks + cubes + 3,)),
+            dma((2, cubes)),
+            pltpu.VMEM((blocks + 1, width, width), F32),
+            pltpu.VMEM((blocks + 1, max(width, staging), width), BF),
+            pltpu.VMEM((blocks + 1, width, width), BF),
+            pltpu.VMEM((blocks + 1, staging, width), BF),
+            pltpu.VMEM((blocks + 1, kept, width), BF),
+            (dma((2 * blocks + 2,)), dma((2 * blocks + 2,))),
+            (dma((blocks + 1, PARTS, 2 * stages + 1)), dma((blocks + 1, PARTS, 2 * stages + 1))),
+            pltpu.VMEM((3, width, half), F32),
+            pltpu.VMEM((8, width), F32),
+            pltpu.VMEM((3, staging, half), BF),
+            pltpu.VMEM((3, staging, half), BF),
+            pltpu.VMEM((3, kept_qkv, half), BF),
+            tuple(pltpu.VMEM((1 << len(names), 8, width), F32) for names in small),
+            (dma((3, 2 * stages + 1)), dma((3, 2 * stages + 1))),
+            (dma((1,)), dma((1,))),
+            (dma((len(small), 8)), dma((len(small), 8))),
+            pltpu.VMEM((groups, half, 2 * cap), BF),
             pltpu.VMEM((packs, 256, wide), BF),
             pltpu.VMEM((packs, 256, wide), BF),
-            pltpu.VMEM((groups, groups * cap, width), BF),
             pltpu.VMEM((groups, half, 2 * cap), BF),
-            pltpu.VMEM((cubes, quarter, width), F32),
-            block, block, block, block, block, block,
-            pair, pair, pair, pair,
+            rows, rows, rows,
+            pair, pair, pair,
         ],
         compiler_params=pltpu.CompilerParams(
-            collective_id=1, has_side_effects=True, vmem_limit_bytes=60 * 2**20),
-        name="backward",
-    )(grad_att, kv, kaug, qt, ot, lse, normed, dest, w_qkv, enc, visible, mask_token, gain, grad_middle)
+            collective_id=1, has_side_effects=True, vmem_limit_bytes=63 * 2**20),
+        name="layer",
+    )(att, kv, kaug, qt, ot, lse, normed, dest, w_qkv, enc, visible, mask_token, gain,
+      cot, w_out, w_up, w_down, gain2, offset2)
+
+
+def cast_kernel(ups, downs, outs, qkvs, up, down, out, qkv):
+    width, half = outs.shape[1], qkvs.shape[3]
+    for k in range(ups.shape[0]):
+        up[:, k * width:(k + 1) * width] = ups[k].astype(F32)
+    down[...] = downs[...].astype(F32)
+    out[...] = outs[...].astype(F32)
+    for part in range(3):
+        for side in range(2):
+            at = part * width + side * half
+            qkv[:, at:at + half] = qkvs[side, part].astype(F32)
+
+
+def cast_call(ffn, qkv):
+    width = qkv.shape[2]
+    blocks = ffn.shape[0] // (2 * width)
+    steps = 8
+    rows = width // steps
+    tall = blocks * rows
+    shape = jax.ShapeDtypeStruct
+    return pl.pallas_call(
+        cast_kernel,
+        grid=(steps,),
+        in_specs=[
+            pl.BlockSpec((blocks, rows, width), lambda i: (0, i, 0)),
+            pl.BlockSpec((tall, width), lambda i: (steps + i, 0)),
+            pl.BlockSpec((rows, width), lambda i: (2 * blocks * steps + i, 0)),
+            pl.BlockSpec((2, 3, rows, width // 2), lambda i: (0, 0, i, 0)),
+        ],
+        out_specs=[
+            pl.BlockSpec((rows, blocks * width), lambda i: (i, 0)),
+            pl.BlockSpec((tall, width), lambda i: (i, 0)),
+            pl.BlockSpec((rows, width), lambda i: (i, 0)),
+            pl.BlockSpec((rows, 3 * width), lambda i: (i, 0)),
+        ],
+        out_shape=(
+            shape((width, blocks * width), F32),
+            shape((blocks * width, width), F32),
+            shape((width, width), F32),
+            shape((width, 3 * width), F32),
+        ),
+        name="cast",
+    )(ffn.reshape(2 * blocks + 1, width, width), ffn, ffn, qkv)
 
 
 def on_device(
@@ -463,7 +1038,6 @@
 ):
     groups = lax.axis_size("group")
     tok_dev, width = enc.shape
-    half = width // 2
     quarter = CUBE_TOK // groups
     cubes = tok_dev // quarter
     column = visible.reshape(tok_dev, 1)
@@ -471,38 +1045,12 @@
     gain1, mask_row = ln1_gain[None, :], mask_token[None, :]
     att, normed, dest, kv, kaug, qt, ot, lse = forward_call(
         enc, column, ids, gain1, ln1_bias[None, :], mask_row, w_qkv, cubes, groups)
-    attended = att.transpose(0, 2, 1).reshape(tok_dev, width)
-    start_rows = jnp.where(column == 1, enc.astype(F32), mask_row)
-    middle = start_rows + dot(attended, w_out)
-    normal2, recip2 = norm_stats(middle)
-    second = (normal2 * ln2_gain + ln2_bias).astype(BF)
-    hidden = dot(second, w_up)
-    active_full, gelu_pull = jax.vjp(lambda v: jax.nn.gelu(v, approximate=True), hidden)
-    active = active_full.astype(BF)
-    out = (middle + dot(active, w_down)).astype(BF)
-    grad_w_down = dot(active, cotangent, TN)
-    grad_hidden = gelu_pull(dot(cotangent, w_down, NT))[0].astype(BF)
-    grad_w_up = dot(second, grad_hidden, TN)
-    grad_second = dot(grad_hidden, w_up, NT)
-    grad_ln2_gain = jnp.sum(grad_second * normal2, axis=0)
-    grad_ln2_bias = jnp.sum(grad_second, axis=0)
-    grad_middle = cotangent.astype(F32) + norm_back(grad_second, normal2, recip2, ln2_gain)
-    grad_branch = grad_middle.astype(BF)
-    grad_w_out = dot(attended, grad_branch, TN)
-    grad_attended = dot(w_out, grad_branch, NT).astype(BF)
-    grad_att = grad_attended.reshape(width, cubes, quarter).transpose(1, 0, 2)
-    grad_enc, grad_qkv, small = backward_call(
-        grad_att, kv, kaug, qt, ot, lse, normed, dest, w_qkv, enc, column, mask_row, gain1, grad_middle)
-    parity = lax.rem(lax.axis_index("group"), 2)
-    mine = grad_qkv.reshape(width, 3, 1, half)
-    blank = jnp.zeros_like(mine)
-    grad_w_qkv = jnp.where(
-        parity == 0, jnp.concatenate([mine, blank], axis=2), jnp.concatenate([blank, mine], axis=2)
-    ).reshape(width, 3 * width)
-    summed = lax.psum(
-        (small[0], small[1], grad_w_qkv, grad_w_out, grad_ln2_gain, grad_ln2_bias, grad_w_up,
-         grad_w_down, small[2]), ("dp", "group"))
-    return (out, grad_enc) + tuple(summed)
+    out, grad_enc, sum_ffn, sum_qkv, small = layer_call(
+        att, kv, kaug, qt, ot, lse, normed, dest, w_qkv, enc, column, mask_row, gain1, cotangent, w_out, w_up,
+        w_down, ln2_gain[None, :], ln2_bias[None, :], lax.axis_size("dp"), groups)
+    sum_up, sum_down, sum_out, sum_w_qkv = cast_call(sum_ffn.reshape(9 * width, width), sum_qkv)
+    return (
+        out, grad_enc, small[0], small[1], sum_w_qkv, sum_out, small[3], small[4], sum_up, sum_down, small[2])
 
 
 def solution(mesh):

time: 428 us -> 211 us (0.49)
  waiting for transfers between devices: 183 us -> 0 us
  Pallas kernels: 122 us -> 202 us
  blocking collectives: 42.2 us -> 0 us
  matrix products: 38.3 us -> 0 us
  local copies, waits for them, and re-layouts: 24.5 us -> 7.25 us
  between operations: 14.2 us -> 0.67 us
    psum x1 -> x0, waiting for transfers between devices: 182 us -> none  [on_device(): lax.psum((small[0], small[1], grad_w_qkv, grad_w_out, grad_ln2_gain, grad...]
    pallas_call x1 -> x2, Pallas kernels: 71.8 us -> 157 us  [the longest x1 148 us: layer_call(): pl.pallas_call(functools.partial(layer_kernel, n_dp, n_group), out_shape=...]
    psum x1 -> x0, blocking collectives: 42.2 us -> none  [on_device(): lax.psum((small[0], small[1], grad_w_qkv, grad_w_out, grad_ln2_gain, grad...]
    dot_general x9 -> x0, matrix products: 38.3 us -> none  [dot(): return lax.dot_general(left, right, dims, preferred_element_type=F32)]
    unnamed x41 -> x6, local copies, waits for them, and re-layouts: 12.9 us -> 2.71 us
    pallas_call x1, Pallas kernels: 50.5 us -> 45.1 us  [forward_call(): pl.pallas_call(forward_kernel, out_shape=(shape((cubes, width, quarter),...]
  transfers between devices with their start and end apart: 1 -> 0, of which waited for: 1 -> 0; matrix products, arithmetic and copies ran while one was open for 2% -> 0% of each run, Pallas kernels for 0% -> 0%
where the time goes in v2:
time: 211 us; the launch traced here: 210 us
  Pallas kernels  202 us (96%)
  local copies, waits for them, and re-layouts  7.25 us (3%)
    pallas_call x1, Pallas kernels, layer_call(): pl.pallas_call(functools.partial(layer_kernel, n_dp, n_group), out_shape=...  148 us
    pallas_call x1, Pallas kernels, forward_call(): pl.pallas_call(forward_kernel, out_shape=(shape((cubes, width, quarter),...  45.1 us
    pallas_call x1, Pallas kernels, cast_call(): pl.pallas_call(cast_kernel, grid=(steps,), in_specs=[pl.BlockSpec((blocks...  8.77 us

profile of v2, /device:TPU:0, one launch (start us, length us, event | category | flops | bytes accessed | tf_op | source)
XLA Modules:
  0.0 210.0 jit_solution(14331766125889048217)
XLA Ops:
  0.6 0.7 reshape.32
  1.3 0.6 pad.4.ids
  2.0 1.7 reshape.34.visible
  3.7 45.1 %forward.1 = (bf16[3,512,384]{2,1,0:T(8,128)(2,1)}, bf16[4,3,384,512]{3,2,1,0:T(8,128)(2,1)}, s32[4,8,384]{2,1,0:T(8,128)}, bf16[3,4,512,512]{3,2,1,0:T(8,128)(2...) custom-call(bf16[1152,512]{1,0:T(8,128)(2,1)} %enc.3, ...), custom_call_target="tpu_custom_call" | custom-call | tf_op jit(solution)/shard_map/forward/pallas_call | solution.py:458
  48.8 148.2 %layer.1 = (bf16[1152,512]{1,0:T(8,128)(2,1)}, bf16[1152,512]{1,0:T(8,128)(2,1)}, bf16[9,512,512]{2,1,0:T(8,128)(2,1)}, bf16[2,3,512,256]{3,2,1,0:T(8,128)(2,1)}, f32[8,512]{1,0:T(8,128)}) custom-call(bf16[3,512,384]{2,1,0:T(8,128)(2,1)} %get-tuple-element.28.att_in, bf16[3,4,512,512]{3,2,1,0:T(8,128)(2,1)} %get-tuple-element.29.kv_in, ...), custom_call_target="tpu_custom_call" | custom-call | tf_op jit(solution)/shard_map/layer/pallas_call | solution.py:926
  197.0 1.5 fusion
  198.5 0.0 copy-start.1
  198.5 8.8 %cast.1 = (f32[512,2048]{1,0:T(8,128)}, f32[2048,512]{1,0:T(8,128)}, f32[512,512]{1,0:T(8,128)}, f32[512,1536]{1,0:T(8,128)}) custom-call(bf16[9,512,512]{2,1,0:T(8,128)(2,1)} %get-tuple-element.39.ups, bf16[4608,512]{1,0:T(8,128)(2,1)} %bitcast.11, bf16[4608,512]{1,0:T(8,128)(2,1)} %bitcast.12, bf16[2,3,512,256]{3,2,1,0:T(8,128)(2,1)} %get-tuple-element.40.qkvs), custom_call_target="tpu_custom_call" | custom-call | tf_op jit(solution)/shard_map/cast/pallas_call | solution.py:1010
  207.2 0.0 copy-start
  207.2 0.0 copy-done.1
  207.3 1.0 copy.28
  208.3 0.7 copy-done
  208.9 1.0 copy.29
Async XLA Ops:
  198.5 8.8 %copy-start.1 = (bf16[1152,512]{1,0:T(8,128)(2,1)S(1)}, bf16[1152,512]{1,0:T(8,128)(2,1)}, u32[]{:S(2)}) copy-start(bf16[1152,512]{1,0:T(8,128)(2,1)} %get-tuple-element.61) | copy-start | bytes 3538948
  207.2 1.7 copy-start

commit v3 on v2

--- a/solution.py
+++ b/solution.py
@@ -107,7 +107,16 @@
         self.sems, self.names = sems, names
         self.rows = acc.shape[0]
         self.halvings = halvings_of(self.rows, len(names))
-        self.stages = len(names)
+        self.groups = [[name] for name in names]
+        if self.halvings >= 4:
+            last = names[self.halvings - 2:self.halvings]
+            self.groups[self.halvings - 2:self.halvings] = [last]
+        self.legs = sum((1 << len(group)) - 1 for group in self.groups)
+        self.halving_groups = [
+            g for g in range(len(self.groups)) if self.done(g) < self.halvings]
+
+    def done(self, g):
+        return sum(len(group) for group in self.groups[:g])
 
     def start_row(self, k):
         low = 0
@@ -118,49 +127,68 @@
     def span(self, low, count):
         return pl.ds(pl.multiple_of(low, 16), count)
 
-    def hop(self, k):
-        if k < self.halvings:
-            count = self.rows >> (k + 1)
-            at = self.rows - (self.rows >> k)
+    def partners(self, g):
+        names, done = self.groups[g], self.done(g)
+        number = sum((1 << len(group)) - 1 for group in self.groups[:g])
+        found = []
+        for t in range(1, 1 << len(names)):
+            low = self.start_row(done)
+            if done < self.halvings:
+                for k, name in enumerate(names):
+                    value = 1 - bit_value(name) if (t >> k) & 1 else bit_value(name)
+                    low = low + value * (self.rows >> (done + k + 1))
+            found.append(([name for k, name in enumerate(names) if (t >> k) & 1], number + t - 1, low))
+        return found
+
+    def hops(self, g):
+        done, size = self.done(g), len(self.groups[g])
+        if done < self.halvings:
+            count = self.rows >> (done + size)
+            at = self.rows - (self.rows >> done)
         else:
             count = self.rows >> self.halvings
-            at = self.rows + (k - self.halvings - 1) * count
-        where = pl.ds(at, count)
-        return copy_to(self.send.at[where], self.recv.at[where], self.sems, k, flip([self.names[k]])), where, count
-
-    def reduce_start(self, k):
-        item, where, count = self.hop(k)
-        low = self.start_row(k)
-        if k < self.halvings:
-            low = low + (1 - bit_value(self.names[k])) * count
-        self.send[where, :] = self.acc[self.span(low, count), :].astype(BF)
-        item.start()
-
-    def reduce_finish(self, k):
-        item, where, count = self.hop(k)
-        item.wait()
-        if k < self.halvings:
-            rows = self.span(self.start_row(k + 1), count)
-            self.acc[rows, :] += self.recv[where, :].astype(F32)
-        else:
-            rows = self.span(self.start_row(k), count)
-            self.acc[rows, :] = self.send[where, :].astype(F32) + self.recv[where, :].astype(F32)
+            at = self.rows + (done - self.halvings - 1) * count
+        found = []
+        for n, (names, number, low) in enumerate(self.partners(g)):
+            where = pl.ds(at + n * count, count)
+            item = copy_to(self.send.at[where], self.recv.at[where], self.sems, number, flip(names))
+            found.append((item, where, self.span(low, count)))
+        return found, count
+
+    def reduce_start(self, g):
+        for item, where, rows in self.hops(g)[0]:
+            self.send[where, :] = self.acc[rows, :].astype(BF)
+            item.start()
+
+    def reduce_finish(self, g):
+        found, count = self.hops(g)
+        rows = self.span(self.start_row(self.done(g) + len(self.groups[g])), count)
+        for item, where, _ in found:
+            item.wait()
+        for _, where, _ in found:
+            if self.done(g) < self.halvings:
+                self.acc[rows, :] += self.recv[where, :].astype(F32)
+            else:
+                self.acc[rows, :] = self.send[where, :].astype(F32) + self.recv[where, :].astype(F32)
 
     def own_piece(self):
         return self.span(self.start_row(self.halvings), self.rows >> self.halvings)
 
     def keep(self):
         return pltpu.make_async_copy(
-            self.settled, self.out.at[self.own_piece(), :], self.sems[0].at[self.stages + self.halvings])
+            self.settled, self.out.at[self.own_piece(), :], self.sems[0].at[2 * self.legs])
 
     def settle(self):
         self.settled[...] = self.acc[self.own_piece(), :].astype(BF)
         self.keep().start()
 
-    def gather(self, k):
-        rows = self.span(self.start_row(k + 1), self.rows >> (k + 1))
-        src = self.settled if k == self.halvings - 1 else self.out.at[rows, :]
-        return copy_to(src, self.out.at[rows, :], self.sems, self.stages + k, flip([self.names[k]]))
+    def gather(self, g):
+        done = self.done(g) + len(self.groups[g])
+        rows = self.span(self.start_row(done), self.rows >> done)
+        src = self.settled if done == self.halvings else self.out.at[rows, :]
+        return [
+            copy_to(src, self.out.at[rows, :], self.sems, self.legs + number, flip(names))
+            for names, number, _ in self.partners(g)]
 
 
 def halvings_of(rows, stages):
@@ -176,19 +204,19 @@
 
 
 def reduce_steps(butterflies):
-    stages = butterflies[0].stages
+    stages = len(butterflies[0].groups)
 
     def first():
         for b in butterflies:
             b.reduce_start(0)
 
     steps = [first]
-    for k in range(stages):
-        def step(k=k):
+    for g in range(stages):
+        def step(g=g):
             for b in butterflies:
-                b.reduce_finish(k)
-                if k + 1 < stages:
-                    b.reduce_start(k + 1)
+                b.reduce_finish(g)
+                if g + 1 < stages:
+                    b.reduce_start(g + 1)
                 else:
                     b.settle()
         steps.append(step)
@@ -196,22 +224,26 @@
 
 
 def gather_steps(butterflies):
-    halvings = max(b.halvings for b in butterflies)
+    last = butterflies[0].halving_groups[-1]
+
+    def start(b, g):
+        for item in b.gather(g):
+            item.start()
 
     def first():
         for b in butterflies:
-            b.gather(b.halvings - 1).start()
+            start(b, last)
 
     steps = [first]
-    for k in range(halvings - 1, -1, -1):
-        def step(k=k):
+    for g in range(last, -1, -1):
+        def step(g=g):
             for b in butterflies:
-                if k < b.halvings:
-                    b.gather(k).wait()
-                    if k == b.halvings - 1:
-                        b.keep().wait()
-                    if k > 0:
-                        b.gather(k - 1).start()
+                for item in b.gather(g):
+                    item.wait()
+                if g == last:
+                    b.keep().wait()
+                if g > 0:
+                    start(b, g - 1)
         steps.append(step)
     return steps
 
@@ -227,6 +259,11 @@
 def path_orders(names, count):
     head, tail = names[:count], names[count:]
     return [head[k:] + head[:k] + tail for k in range(count)]
+
+
+def balanced_orders(names):
+    first, second, third, tail = names[0], names[1], names[2], names[3:]
+    return [[second, first, third] + tail, [second, third, first] + tail] + [[third, second, first] + tail] * 2
 
 
 def chip_bits(n_dp, n_group):
@@ -280,11 +317,18 @@
         return total
 
 
+def as_columns(codes, columns):
+    shown = jnp.where(codes[...] >= 8, 1.0, 0.0)
+    shown = jnp.concatenate([shown, jnp.zeros((8 - shown.shape[0], shown.shape[1]), F32)], axis=0).T
+    for c in range(codes.shape[0]):
+        columns[c] = shown[:, c:c + 1]
+
+
 def forward_kernel(
-    enc, visible, ids, gain, offset, mask_token, w_qkv,
+    enc, codes, gain, offset, mask_token, w_qkv,
     att, normed_out, dest, kv_out, kaug_out, qt_out, ot_out, lse,
     sems_load,
-    normed, kv, kaug, qt, ot, w_mine, wq_t, qbd, vt, away, sems_in, sems_dest, sems_fwd, sems_att, sems_store,
+    normed, kv, kaug, qt, ot, columns, w_mine, wq_t, qbd, vt, away, sems_in, sems_dest, sems_fwd, sems_att, sems_store,
 ):
     cubes, quarter = normed.shape[1], normed.shape[2]
     width = enc.shape[1]
@@ -309,7 +353,9 @@
 
     greet([sibling, across, cross])
 
-    dest[0] = own_dest(ids[...], cap, groups)
+    dest[0] = jnp.zeros(dest.shape[1:], jnp.int32)
+    dest[0, :cubes] = own_dest(codes[...] & 7, cap, groups)
+    as_columns(codes, columns)
     to_peers = []
     for index, device in enumerate((sibling, across, cross)):
         item = copy_to(dest.at[0], dest.at[index + 1], sems_dest, index, device)
@@ -318,8 +364,7 @@
 
     def start_rows(c):
         rows = enc[pl.ds(c * quarter, quarter), :].astype(F32)
-        shown = visible[pl.ds(c * quarter, quarter), :] == 1
-        return jnp.where(shown, rows, mask_token[...])
+        return jnp.where(columns[c] == 1.0, rows, mask_token[...])
 
     def own_rows(c, _):
         normal, _ = norm_stats(start_rows(c))
@@ -444,7 +489,7 @@
         item.wait_send()
 
 
-def forward_call(enc, visible, ids, gain, offset, mask_token, w_qkv, cubes, groups):
+def forward_call(enc, codes, gain, offset, mask_token, w_qkv, cubes, groups):
     tokens, width = enc.shape
     quarter = tokens // cubes
     cap = quarter // 3
@@ -467,7 +512,7 @@
             shape((cubes, groups, half, 2 * cap), BF),
             shape((cubes, groups, 8, wide), F32),
         ),
-        in_specs=[vmem] * 6 + [far],
+        in_specs=[vmem] * 5 + [far],
         out_specs=(vmem, far, vmem, far, far, far, far, vmem),
         scratch_shapes=[
             dma((3,)),
@@ -476,6 +521,7 @@
             pltpu.VMEM((cubes, groups, groups * cap, 128), BF),
             pltpu.VMEM((cubes, groups, half, 2 * cap), BF),
             pltpu.VMEM((cubes, groups, half, 2 * cap), BF),
+            pltpu.VMEM((cubes, quarter, 1), F32),
             pltpu.VMEM((width, 3 * half), BF),
             pltpu.VMEM((half, width), BF),
             pltpu.VMEM((packs, 256, wide), BF),
@@ -490,7 +536,7 @@
         compiler_params=pltpu.CompilerParams(
             collective_id=0, has_side_effects=True, vmem_limit_bytes=60 * 2**20),
         name="forward",
-    )(enc, visible, ids, gain, offset, mask_token, w_qkv)
+    )(enc, codes, gain, offset, mask_token, w_qkv)
 
 
 def pieces(values):
@@ -510,7 +556,7 @@
     cot, w_out, w_up, w_down, att, middle, second, backs, result, grads_sum, spare, w_mine, sems_load, sems_out,
     acc, give, pair, recv, settled, sems_core, sems_ffn,
     grad_qkv, small, send_qkv, recv_qkv, settled_qkv, small_bufs, sems_qkv, sems_pair, sems_small,
-    dot_slots, qbd, dobd, grad_qt, in_sib, in_fwd, in_across, sems_sib, sems_fwd, sems_across,
+    columns, dot_slots, qbd, dobd, grad_qt, in_sib, in_fwd, in_across, sems_sib, sems_fwd, sems_across,
 ):
     cubes, quarter, width = middle.shape
     half = width // 2
@@ -531,7 +577,7 @@
 
     core = ("group", 1)
     others = chip_bits(n_dp, n_group)
-    paths = path_orders(others, PARTS)
+    paths = balanced_orders(others)
     qkv = [
         Butterfly(grad_qkv.at[p], send_qkv.at[p], recv_qkv.at[p], settled_qkv.at[p], sum_qkv.at[parity, p],
                   (sems_qkv[0].at[p], sems_qkv[1].at[p]), order)
@@ -610,15 +656,17 @@
     for names in small_groups(n_dp, n_group):
         for t in range(1, 1 << len(names)):
             chosen = [name for k, name in enumerate(names) if (t >> k) & 1]
-            meets[tuple(chosen)] = flip(chosen)
-    for name in [core] + others:
-        meets[(name,)] = flip([name])
+            meets[tuple(sorted(chosen))] = flip(chosen)
+    for chosen in [[core]] + [[name] for name in others] + [
+            list(pair) for i, first in enumerate(others) for pair in ((first, other) for other in others[i + 1:])]:
+        meets[tuple(sorted(chosen))] = flip(chosen)
     greet(list(meets.values()))
 
     one_row = lax.broadcasted_iota(jnp.int32, (16, per * 2 * cap), 0)
     for p in range(packs):
         qbd[p] = jnp.zeros(qbd.shape[1:], BF)
         dobd[p] = jnp.zeros(dobd.shape[1:], BF)
+    as_columns(visible, columns)
     grad_qkv[...] = jnp.zeros(grad_qkv.shape, F32)
     small[...] = jnp.zeros(small.shape, F32)
 
@@ -626,7 +674,7 @@
         return pl.ds(c * quarter, quarter)
 
     def start_rows(c):
-        shown = visible[rows_of(c), :] == 1
+        shown = columns[c] == 1.0
         return shown, jnp.where(shown, enc[rows_of(c), :].astype(F32), mask_token[...])
 
     def turn_copy(c):
@@ -709,9 +757,11 @@
             if at == place:
                 step()
 
-    for item in loads:
+    for item in loads[:2]:
         item.wait()
     lax.fori_loop(0, cubes, enter, 0)
+    for item in loads[2:]:
+        item.wait()
     place = blocks * cubes
 
     def blocks_step(u, _):
@@ -771,7 +821,7 @@
                 cols = slice(j * 2 * cap, (j + 1) * 2 * cap)
                 grad_qt[s, rows, :] = mixed[j * hd:(j + 1) * hd, cols].astype(BF)
 
-    def back_project(r, c):
+    def back_rows(r, c):
         hot = onehot(dest[r, pl.ds(c, 1), :], slots)
         placed = jnp.concatenate(
             [grad_kv[s, r * cap:(r + 1) * cap, :] for s in range(groups)], axis=0)
@@ -781,14 +831,15 @@
                 [grad_qt[s, :, r * cap:(r + 1) * cap] for s in range(groups)], axis=1)
             queries = dot(queries, hot).T.astype(BF)
             grads = jnp.concatenate([queries, grads], axis=1)
-            weight = dot(normed_at[lax.rem(c, 2), r], grads, TN)
-            for k in range(3):
-                grad_qkv[k] += weight[:, k * half:(k + 1) * half]
-            return dot(grads, w_mine[...], NT)
         weight = dot(normed_at[lax.rem(c, 2), r], grads, TN)
-        for k in range(2):
-            grad_qkv[k + 1] += weight[:, k * half:(k + 1) * half]
-        return dot(grads, w_mine[:, half:], NT)
+        first = 3 - weight.shape[1] // half
+        for k in range(first, 3):
+            grad_qkv[k] += weight[:, (k - first) * half:(k - first + 1) * half]
+        return grads
+
+    def back_project(r, c):
+        grads = back_rows(r, c)
+        return dot(grads, w_mine[:, 3 * half - grads.shape[1]:], NT)
 
     def prepare(c):
         for item in reads(c):
@@ -826,10 +877,13 @@
         out_across[c] = (partial + in_fwd[c].astype(F32)).astype(BF)
         copy_to(out_across.at[c], in_across.at[c], sems_across, c, across).start()
         point(6)
-        out_sib[c] = back_project(1, c).astype(BF)
+        near_rows = back_rows(1, c)
+        own_rows = back_rows(0, c)
+        pl.when(c == cubes - 1)(qkv_steps[0])
+        point(7)
+        out_sib[c] = dot(near_rows, w_mine[...], NT).astype(BF)
         copy_to(out_sib.at[c], in_sib.at[c], sems_sib, c, sibling).start()
-        point(7)
-        own_sum[c] = back_project(0, c)
+        own_sum[c] = dot(own_rows, w_mine[...], NT)
 
         def more():
             for item in reads(c + 2):
@@ -840,7 +894,6 @@
         return 0
 
     lax.fori_loop(0, cubes, cube, 0)
-    qkv_steps[0]()
     tail = [(at - lead - POINTS * cubes, step) for at, step in plan if at > lead + POINTS * cubes]
 
     def last(c):
@@ -858,23 +911,36 @@
         small[2:3, :] += jnp.sum(jnp.where(shown, 0.0, total), axis=0, keepdims=True)
 
     fill = list(range(cubes))
+    pending = []
+
+    def small_step():
+        total = smalls[pending[0]].finish()
+        pending.append(pending.pop(0) + 1)
+        if pending[0] < len(smalls):
+            smalls[pending[0]].start(total)
+        else:
+            pending.clear()
+            sum_small[...] = total
+
     for k in range(1, len(qkv_steps)):
         if fill:
             last(fill.pop(0))
             if not fill:
                 smalls[0].start(small[...])
-        qkv_steps[k]()
+                pending.append(0)
+            qkv_steps[k]()
+        else:
+            qkv_steps[k]()
+            if pending:
+                small_step()
         while tail and tail[0][0] <= k:
             tail.pop(0)[1]()
     pair_qkv = copy_to(sum_qkv.at[parity], sum_qkv.at[parity], sems_pair, 0, sibling)
     pair_qkv.start()
     for _, step in tail:
         step()
-    for k, item in enumerate(smalls):
-        total = item.finish()
-        if k + 1 < len(smalls):
-            smalls[k + 1].start(total)
-    sum_small[...] = total
+    while pending:
+        small_step()
     for c in range(cubes):
         enc_copy(c).wait()
     pair_qkv.wait()
@@ -883,19 +949,19 @@
 POINTS = 9
 PARTS = 4
 SUM_AT = [
-    [3, 5, 9, 12, 16, 19],
-    [6, 8, 12, 16, 19, 21],
-    [9, 11, 15, 19, 22, 25],
-    [12, 14, 18, 20, 22, 25],
-    [16, 18, 21, 25, 28, 32],
+    [3, 5, 9, 12, 16],
+    [6, 8, 12, 17, 20],
+    [9, 11, 15, 19, 22],
+    [12, 14, 18, 21, 25],
+    [16, 18, 21, 26, 29],
 ]
 SPREADS = [[0], [1], [2], [3], [4]]
 SPREAD_AT = [
-    [19, 21, 24, 27, 30, 32],
-    [21, 24, 27, 31, 35, 37],
-    [25, 28, 31, 36, 39, 41],
-    [25, 28, 32, 37, 41, 43],
-    [32, 37, 41, 44, 46, 47],
+    [16, 20, 23, 28, 30],
+    [20, 24, 28, 32, 34],
+    [22, 27, 30, 35, 37],
+    [25, 29, 33, 37, 39],
+    [29, 33, 37, 39, 41],
 ]
 
 
@@ -964,16 +1030,17 @@
             pltpu.VMEM((blocks + 1, staging, width), BF),
             pltpu.VMEM((blocks + 1, kept, width), BF),
             (dma((2 * blocks + 2,)), dma((2 * blocks + 2,))),
-            (dma((blocks + 1, PARTS, 2 * stages + 1)), dma((blocks + 1, PARTS, 2 * stages + 1))),
+            (dma((blocks + 1, PARTS, 2 * stages + 3)), dma((blocks + 1, PARTS, 2 * stages + 3))),
             pltpu.VMEM((3, width, half), F32),
             pltpu.VMEM((8, width), F32),
             pltpu.VMEM((3, staging, half), BF),
             pltpu.VMEM((3, staging, half), BF),
             pltpu.VMEM((3, kept_qkv, half), BF),
             tuple(pltpu.VMEM((1 << len(names), 8, width), F32) for names in small),
-            (dma((3, 2 * stages + 1)), dma((3, 2 * stages + 1))),
+            (dma((3, 2 * stages + 3)), dma((3, 2 * stages + 3))),
             (dma((1,)), dma((1,))),
             (dma((len(small), 8)), dma((len(small), 8))),
+            pltpu.VMEM((cubes, quarter, 1), F32),
             pltpu.VMEM((groups, half, 2 * cap), BF),
             pltpu.VMEM((packs, 256, wide), BF),
             pltpu.VMEM((packs, 256, wide), BF),
@@ -1003,7 +1070,7 @@
 def cast_call(ffn, qkv):
     width = qkv.shape[2]
     blocks = ffn.shape[0] // (2 * width)
-    steps = 8
+    steps = 2
     rows = width // steps
     tall = blocks * rows
     shape = jax.ShapeDtypeStruct
@@ -1040,13 +1107,12 @@
     tok_dev, width = enc.shape
     quarter = CUBE_TOK // groups
     cubes = tok_dev // quarter
-    column = visible.reshape(tok_dev, 1)
-    ids = jnp.pad(band_group.reshape(cubes, quarter), ((0, 8 - cubes), (0, 0)), constant_values=-1)
+    codes = (visible * 8 + band_group).reshape(cubes, quarter)
     gain1, mask_row = ln1_gain[None, :], mask_token[None, :]
     att, normed, dest, kv, kaug, qt, ot, lse = forward_call(
-        enc, column, ids, gain1, ln1_bias[None, :], mask_row, w_qkv, cubes, groups)
+        enc, codes, gain1, ln1_bias[None, :], mask_row, w_qkv, cubes, groups)
     out, grad_enc, sum_ffn, sum_qkv, small = layer_call(
-        att, kv, kaug, qt, ot, lse, normed, dest, w_qkv, enc, column, mask_row, gain1, cotangent, w_out, w_up,
+        att, kv, kaug, qt, ot, lse, normed, dest, w_qkv, enc, codes, mask_row, gain1, cotangent, w_out, w_up,
         w_down, ln2_gain[None, :], ln2_bias[None, :], lax.axis_size("dp"), groups)
     sum_up, sum_down, sum_out, sum_w_qkv = cast_call(sum_ffn.reshape(9 * width, width), sum_qkv)
     return (

time: 211 us -> 199 us (0.943)
  Pallas kernels: 202 us -> 192 us
  local copies, waits for them, and re-layouts: 7.25 us -> 4.81 us
    pallas_call x1, Pallas kernels: 148 us -> 141 us  [layer_call(): pl.pallas_call(functools.partial(layer_kernel, n_dp, n_group), out_shape=...]
where the time goes in v3:
time: 199 us
  Pallas kernels  192 us (96%)
  local copies, waits for them, and re-layouts  4.81 us (2%)
    pallas_call x1, Pallas kernels, layer_call(): pl.pallas_call(functools.partial(layer_kernel, n_dp, n_group), out_shape=...  141 us
    pallas_call x1, Pallas kernels, forward_call(): pl.pallas_call(forward_kernel, out_shape=(shape((cubes, width, quarter),...  44.9 us
    pallas_call x1, Pallas kernels, cast_call(): pl.pallas_call(cast_kernel, grid=(steps,), in_specs=[pl.BlockSpec((blocks...  6.81 us

profile of v3, /device:TPU:0, one launch (start us, length us, event | category | flops | bytes accessed | tf_op | source)
XLA Modules:
  0.0 198.7 jit_solution(6161270194846375774)
XLA Ops:
  0.6 0.7 multiply_add_fusion
  1.4 0.6 reshape.28.codes.visible
  2.0 44.9 %forward.1 = (bf16[3,512,384]{2,1,0:T(8,128)(2,1)}, bf16[4,3,384,512]{3,2,1,0:T(8,128)(2,1)}, s32[4,8,384]{2,1,0:T(8,128)}, bf16[3,4,512,512]{3,2,1,0:T(8,128)(2...) custom-call(bf16[1152,512]{1,0:T(8,128)(2,1)} %enc.3, ...), custom_call_target="tpu_custom_call" | custom-call | tf_op jit(solution)/shard_map/forward/pallas_call | solution.py:503
  46.9 140.7 %layer.1 = (bf16[1152,512]{1,0:T(8,128)(2,1)}, bf16[1152,512]{1,0:T(8,128)(2,1)}, bf16[9,512,512]{2,1,0:T(8,128)(2,1)}, bf16[2,3,512,256]{3,2,1,0:T(8,128)(2,1)}, f32[8,512]{1,0:T(8,128)}) custom-call(bf16[3,512,384]{2,1,0:T(8,128)(2,1)} %get-tuple-element.28.att_in, bf16[3,4,512,512]{3,2,1,0:T(8,128)(2,1)} %get-tuple-element.29.kv_in, ...), custom_call_target="tpu_custom_call" | custom-call | tf_op jit(solution)/shard_map/layer/pallas_call | solution.py:992
  187.7 1.5 fusion
  189.2 0.0 copy-start.1
  189.2 6.8 %cast.1 = (f32[512,2048]{1,0:T(8,128)}, f32[2048,512]{1,0:T(8,128)}, f32[512,512]{1,0:T(8,128)}, f32[512,1536]{1,0:T(8,128)}) custom-call(bf16[9,512,512]{2,1,0:T(8,128)(2,1)} %get-tuple-element.39.ups, bf16[4608,512]{1,0:T(8,128)(2,1)} %bitcast.11, bf16[4608,512]{1,0:T(8,128)(2,1)} %bitcast.12, bf16[2,3,512,256]{3,2,1,0:T(8,128)(2,1)} %get-tuple-element.40.qkvs), custom_call_target="tpu_custom_call" | custom-call | tf_op jit(solution)/shard_map/cast/pallas_call | solution.py:1077
  196.0 0.0 copy-start
  196.0 0.0 copy-done.1
  196.0 1.0 copy.26
  197.0 0.7 copy-done
  197.7 1.0 copy.27
Async XLA Ops:
  189.2 6.8 %copy-start.1 = (bf16[1152,512]{1,0:T(8,128)(2,1)S(1)}, bf16[1152,512]{1,0:T(8,128)(2,1)}, u32[]{:S(2)}) copy-start(bf16[1152,512]{1,0:T(8,128)(2,1)} %get-tuple-element.61) | copy-start | bytes 3538948
  196.0 1.7 copy-start

commit v4 on v3

--- a/solution.py
+++ b/solution.py
@@ -581,8 +581,17 @@
     qkv = [
         Butterfly(grad_qkv.at[p], send_qkv.at[p], recv_qkv.at[p], settled_qkv.at[p], sum_qkv.at[parity, p],
                   (sems_qkv[0].at[p], sems_qkv[1].at[p]), order)
-        for p, order in enumerate(path_orders(others, 3))]
+        for p, order in enumerate([balanced_orders(others)[k] for k in (0, 2, 1)])]
     qkv_steps = joined(reduce_steps(qkv), gather_steps(qkv))
+
+    def swap_copies(side):
+        items = []
+        for p, b in enumerate(qkv):
+            count = b.rows // 2
+            value = bit_value(b.names[0])
+            rows = b.out.at[b.span((value if side == 0 else 1 - value) * count, count), :]
+            items.append(copy_to(rows, rows, sems_pair, 3 * side + p, sibling))
+        return items
     smalls = [
         SmallSum(small_bufs[k], (sems_small[0].at[k], sems_small[1].at[k]), names)
         for k, names in enumerate(small_groups(n_dp, n_group))]
@@ -931,19 +940,23 @@
             qkv_steps[k]()
         else:
             qkv_steps[k]()
+            if k == len(qkv_steps) - 2:
+                for item in swap_copies(0):
+                    item.start()
             if pending:
                 small_step()
         while tail and tail[0][0] <= k:
             tail.pop(0)[1]()
-    pair_qkv = copy_to(sum_qkv.at[parity], sum_qkv.at[parity], sems_pair, 0, sibling)
-    pair_qkv.start()
+    for item in swap_copies(1):
+        item.start()
     for _, step in tail:
         step()
     while pending:
         small_step()
     for c in range(cubes):
         enc_copy(c).wait()
-    pair_qkv.wait()
+    for item in swap_copies(0) + swap_copies(1):
+        item.wait()
 
 
 POINTS = 9
@@ -1038,7 +1051,7 @@
             pltpu.VMEM((3, kept_qkv, half), BF),
             tuple(pltpu.VMEM((1 << len(names), 8, width), F32) for names in small),
             (dma((3, 2 * stages + 3)), dma((3, 2 * stages + 3))),
-            (dma((1,)), dma((1,))),
+            (dma((6,)), dma((6,))),
             (dma((len(small), 8)), dma((len(small), 8))),
             pltpu.VMEM((cubes, quarter, 1), F32),
             pltpu.VMEM((groups, half, 2 * cap), BF),
@@ -1055,7 +1068,7 @@
       cot, w_out, w_up, w_down, gain2, offset2)
 
 
-def cast_kernel(ups, downs, outs, qkvs, up, down, out, qkv):
+def cast_kernel(ups, downs, outs, qkvs, small, tokens, grads, up, down, out, qkv, tokens_out, grads_out, *vectors):
     width, half = outs.shape[1], qkvs.shape[3]
     for k in range(ups.shape[0]):
         up[:, k * width:(k + 1) * width] = ups[k].astype(F32)
@@ -1065,14 +1078,19 @@
         for side in range(2):
             at = part * width + side * half
             qkv[:, at:at + half] = qkvs[side, part].astype(F32)
-
-
-def cast_call(ffn, qkv):
+    tokens_out[...] = tokens[...]
+    grads_out[...] = grads[...]
+    for k, vector in enumerate(vectors):
+        vector[...] = small[k:k + 1, :]
+
+
+def cast_call(ffn, qkv, small, tokens, grads):
     width = qkv.shape[2]
     blocks = ffn.shape[0] // (2 * width)
     steps = 2
     rows = width // steps
     tall = blocks * rows
+    token_rows = pl.BlockSpec((tokens.shape[0] // steps, width), lambda i: (i, 0))
     shape = jax.ShapeDtypeStruct
     return pl.pallas_call(
         cast_kernel,
@@ -1082,21 +1100,28 @@
             pl.BlockSpec((tall, width), lambda i: (steps + i, 0)),
             pl.BlockSpec((rows, width), lambda i: (2 * blocks * steps + i, 0)),
             pl.BlockSpec((2, 3, rows, width // 2), lambda i: (0, 0, i, 0)),
+            pl.BlockSpec(small.shape, lambda i: (0, 0)),
+            token_rows,
+            token_rows,
         ],
         out_specs=[
             pl.BlockSpec((rows, blocks * width), lambda i: (i, 0)),
             pl.BlockSpec((tall, width), lambda i: (i, 0)),
             pl.BlockSpec((rows, width), lambda i: (i, 0)),
             pl.BlockSpec((rows, 3 * width), lambda i: (i, 0)),
-        ],
+            token_rows,
+            token_rows,
+        ] + [pl.BlockSpec((1, width), lambda i: (0, 0))] * 5,
         out_shape=(
             shape((width, blocks * width), F32),
             shape((blocks * width, width), F32),
             shape((width, width), F32),
             shape((width, 3 * width), F32),
-        ),
+            shape(tokens.shape, BF),
+            shape(tokens.shape, BF),
+        ) + (shape((1, width), F32),) * 5,
         name="cast",
-    )(ffn.reshape(2 * blocks + 1, width, width), ffn, ffn, qkv)
+    )(ffn.reshape(2 * blocks + 1, width, width), ffn, ffn, qkv, small, tokens, grads)
 
 
 def on_device(
@@ -1114,9 +1139,12 @@
     out, grad_enc, sum_ffn, sum_qkv, small = layer_call(
         att, kv, kaug, qt, ot, lse, normed, dest, w_qkv, enc, codes, mask_row, gain1, cotangent, w_out, w_up,
         w_down, ln2_gain[None, :], ln2_bias[None, :], lax.axis_size("dp"), groups)
-    sum_up, sum_down, sum_out, sum_w_qkv = cast_call(sum_ffn.reshape(9 * width, width), sum_qkv)
+    (sum_up, sum_down, sum_out, sum_w_qkv, out, grad_enc, gain1_sum, bias1_sum, mask_sum, gain2_sum, bias2_sum,
+     ) = cast_call(sum_ffn.reshape(9 * width, width), sum_qkv, small, out, grad_enc)
+    gain1_sum, bias1_sum, mask_sum, gain2_sum, bias2_sum = (
+        vector.reshape(width) for vector in (gain1_sum, bias1_sum, mask_sum, gain2_sum, bias2_sum))
     return (
-        out, grad_enc, small[0], small[1], sum_w_qkv, sum_out, small[3], small[4], sum_up, sum_down, small[2])
+        out, grad_enc, gain1_sum, bias1_sum, sum_w_qkv, sum_out, gain2_sum, bias2_sum, sum_up, sum_down, mask_sum)
 
 
 def solution(mesh):

time: 199 us -> 192 us (0.965)
  local copies, waits for them, and re-layouts: 4.81 us -> 0.6 us
  Pallas kernels: 192 us -> 190 us
    pallas_call x1, Pallas kernels: 141 us -> 137 us  [layer_call(): pl.pallas_call(functools.partial(layer_kernel, n_dp, n_group), out_shape=...]
    unnamed x6 -> x0, local copies, waits for them, and re-layouts: 2.71 us -> none
where the time goes in v4:
time: 192 us
  Pallas kernels  190 us (99%)
    pallas_call x1, Pallas kernels, layer_call(): pl.pallas_call(functools.partial(layer_kernel, n_dp, n_group), out_shape=...  137 us
    pallas_call x1, Pallas kernels, forward_call(): pl.pallas_call(forward_kernel, out_shape=(shape((cubes, width, quarter),...  45 us
    pallas_call x1, Pallas kernels, cast_call(): pl.pallas_call(cast_kernel, grid=(steps,), in_specs=[pl.BlockSpec((blocks...  8.01 us

profile of v4, /device:TPU:0, one launch (start us, length us, event | category | flops | bytes accessed | tf_op | source)
XLA Modules:
  0.0 191.8 jit_solution(4393107292932972439)
XLA Ops:
  0.6 0.7 multiply_add_fusion
  1.4 0.6 reshape.43.codes.visible
  2.0 45.0 %forward.1 = (bf16[3,512,384]{2,1,0:T(8,128)(2,1)}, bf16[4,3,384,512]{3,2,1,0:T(8,128)(2,1)}, s32[4,8,384]{2,1,0:T(8,128)}, bf16[3,4,512,512]{3,2,1,0:T(8,128)(2...) custom-call(bf16[1152,512]{1,0:T(8,128)(2,1)} %enc.3, ...), custom_call_target="tpu_custom_call" | custom-call | tf_op jit(solution)/shard_map/forward/pallas_call | solution.py:503
  46.9 136.6 %layer.1 = (bf16[1152,512]{1,0:T(8,128)(2,1)}, bf16[1152,512]{1,0:T(8,128)(2,1)}, bf16[9,512,512]{2,1,0:T(8,128)(2,1)}, bf16[2,3,512,256]{3,2,1,0:T(8,128)(2,1)}, f32[8,512]{1,0:T(8,128)}) custom-call(bf16[3,512,384]{2,1,0:T(8,128)(2,1)} %get-tuple-element.35.att_in, bf16[3,4,512,512]{3,2,1,0:T(8,128)(2,1)} %get-tuple-element.36.kv_in, ...), custom_call_target="tpu_custom_call" | custom-call | tf_op jit(solution)/shard_map/layer/pallas_call | solution.py:1005
  183.6 8.0 %cast.1 = (f32[512,2048]{1,0:T(8,128)}, f32[2048,512]{1,0:T(8,128)}, f32[512,512]{1,0:T(8,128)}, f32[512,1536]{1,0:T(8,128)}, bf16[1152,512]{1,0:T(8,128)(2,1)},...) custom-call(bf16[9,512,512]{2,1,0:T(8,128)(2,1)} %get-tuple-element., ...), custom_call_target="tpu_custom_call" | custom-call | tf_op jit(solution)/shard_map/cast/pallas_call | solution.py:1095

commit v5 on v4

--- a/solution.py
+++ b/solution.py
@@ -63,10 +63,11 @@
     )
 
 
-def greet(devices):
+def greet(devices, meanwhile):
     barrier = pltpu.get_barrier_semaphore()
     for device in devices:
         pl.semaphore_signal(barrier, inc=1, device_id=device, device_id_type=MESH)
+    meanwhile()
     pl.semaphore_wait(barrier, len(devices))
 
 
@@ -351,29 +352,33 @@
     for item in loads:
         item.start()
 
-    greet([sibling, across, cross])
-
-    dest[0] = jnp.zeros(dest.shape[1:], jnp.int32)
-    dest[0, :cubes] = own_dest(codes[...] & 7, cap, groups)
-    as_columns(codes, columns)
+    def start_rows(c):
+        rows = enc[pl.ds(c * quarter, quarter), :].astype(F32)
+        return jnp.where(columns[c] == 1.0, rows, mask_token[...])
+
+    def own_rows(c, _):
+        normal, _ = norm_stats(start_rows(c))
+        normed[0, c] = (normal * gain[...] + offset[...]).astype(BF)
+        return 0
+
+    def send_rows(c, _):
+        copy_to(normed.at[0, c], normed.at[2, c], sems_in, cubes + c, across).start()
+        copy_to(normed.at[0, c], normed.at[1, c], sems_in, c, sibling).start()
+        return 0
+
+    def before_sending():
+        dest[0] = jnp.zeros(dest.shape[1:], jnp.int32)
+        dest[0, :cubes] = own_dest(codes[...] & 7, cap, groups)
+        as_columns(codes, columns)
+        lax.fori_loop(0, cubes, own_rows, 0)
+
+    greet([sibling, across, cross], before_sending)
+    lax.fori_loop(0, cubes, send_rows, 0)
     to_peers = []
     for index, device in enumerate((sibling, across, cross)):
         item = copy_to(dest.at[0], dest.at[index + 1], sems_dest, index, device)
         item.start()
         to_peers.append(item)
-
-    def start_rows(c):
-        rows = enc[pl.ds(c * quarter, quarter), :].astype(F32)
-        return jnp.where(columns[c] == 1.0, rows, mask_token[...])
-
-    def own_rows(c, _):
-        normal, _ = norm_stats(start_rows(c))
-        normed[0, c] = (normal * gain[...] + offset[...]).astype(BF)
-        copy_to(normed.at[0, c], normed.at[2, c], sems_in, cubes + c, across).start()
-        copy_to(normed.at[0, c], normed.at[1, c], sems_in, c, sibling).start()
-        return 0
-
-    lax.fori_loop(0, cubes, own_rows, 0)
 
     for item in loads:
         item.wait()
@@ -669,16 +674,7 @@
     for chosen in [[core]] + [[name] for name in others] + [
             list(pair) for i, first in enumerate(others) for pair in ((first, other) for other in others[i + 1:])]:
         meets[tuple(sorted(chosen))] = flip(chosen)
-    greet(list(meets.values()))
-
     one_row = lax.broadcasted_iota(jnp.int32, (16, per * 2 * cap), 0)
-    for p in range(packs):
-        qbd[p] = jnp.zeros(qbd.shape[1:], BF)
-        dobd[p] = jnp.zeros(dobd.shape[1:], BF)
-    as_columns(visible, columns)
-    grad_qkv[...] = jnp.zeros(grad_qkv.shape, F32)
-    small[...] = jnp.zeros(small.shape, F32)
-
     def rows_of(c):
         return pl.ds(c * quarter, quarter)
 
@@ -766,9 +762,18 @@
             if at == place:
                 step()
 
-    for item in loads[:2]:
-        item.wait()
-    lax.fori_loop(0, cubes, enter, 0)
+    def before_sums():
+        for p in range(packs):
+            qbd[p] = jnp.zeros(qbd.shape[1:], BF)
+            dobd[p] = jnp.zeros(dobd.shape[1:], BF)
+        as_columns(visible, columns)
+        grad_qkv[...] = jnp.zeros(grad_qkv.shape, F32)
+        small[...] = jnp.zeros(small.shape, F32)
+        for item in loads[:2]:
+            item.wait()
+        lax.fori_loop(0, cubes, enter, 0)
+
+    greet(list(meets.values()), before_sums)
     for item in loads[2:]:
         item.wait()
     place = blocks * cubes

time: 192 us -> 214 us (1.11)
  Pallas kernels: 190 us -> 212 us
    pallas_call x1, Pallas kernels: 45 us -> 68.5 us  [forward_call(): pl.pallas_call(forward_kernel, out_shape=(shape((cubes, width, quarter),...]
where the time goes in v5:
time: 214 us
  Pallas kernels  212 us (99%)
    pallas_call x1, Pallas kernels, layer_call(): pl.pallas_call(functools.partial(layer_kernel, n_dp, n_group), out_shape=...  135 us
    pallas_call x1, Pallas kernels, forward_call(): pl.pallas_call(forward_kernel, out_shape=(shape((cubes, width, quarter),...  68.5 us
    pallas_call x1, Pallas kernels, cast_call(): pl.pallas_call(cast_kernel, grid=(steps,), in_specs=[pl.BlockSpec((blocks...  8.01 us

profile of v5, /device:TPU:0, one launch (start us, length us, event | category | flops | bytes accessed | tf_op | source)
XLA Modules:
  0.0 213.9 jit_solution(9518833343889953)
XLA Ops:
  0.6 0.7 multiply_add_fusion
  1.4 0.6 reshape.43.codes.visible
  2.0 68.5 %forward.1 = (bf16[3,512,384]{2,1,0:T(8,128)(2,1)}, bf16[4,3,384,512]{3,2,1,0:T(8,128)(2,1)}, s32[4,8,384]{2,1,0:T(8,128)}, bf16[3,4,512,512]{3,2,1,0:T(8,128)(2...) custom-call(bf16[1152,512]{1,0:T(8,128)(2,1)} %enc.3, ...), custom_call_target="tpu_custom_call" | custom-call | tf_op jit(solution)/shard_map/forward/pallas_call | solution.py:508
  70.5 135.2 %layer.1 = (bf16[1152,512]{1,0:T(8,128)(2,1)}, bf16[1152,512]{1,0:T(8,128)(2,1)}, bf16[9,512,512]{2,1,0:T(8,128)(2,1)}, bf16[2,3,512,256]{3,2,1,0:T(8,128)(2,1)}, f32[8,512]{1,0:T(8,128)}) custom-call(bf16[3,512,384]{2,1,0:T(8,128)(2,1)} %get-tuple-element.35.att_in, bf16[3,4,512,512]{3,2,1,0:T(8,128)(2,1)} %get-tuple-element.36.kv_in, ...), custom_call_target="tpu_custom_call" | custom-call | tf_op jit(solution)/shard_map/layer/pallas_call | solution.py:1010
  205.8 8.0 %cast.1 = (f32[512,2048]{1,0:T(8,128)}, f32[2048,512]{1,0:T(8,128)}, f32[512,512]{1,0:T(8,128)}, f32[512,1536]{1,0:T(8,128)}, bf16[1152,512]{1,0:T(8,128)(2,1)},...) custom-call(bf16[9,512,512]{2,1,0:T(8,128)(2,1)} %get-tuple-element., ...), custom_call_target="tpu_custom_call" | custom-call | tf_op jit(solution)/shard_map/cast/pallas_call | solution.py:1100
